TPU v7x, 32 devices: a whole 2x2x4 slice. The times are simulated.
32 devices in a mesh: tile: 8 (over z, x), pass: 4 (over y, core).
Axes of the slice: x: 2, y: 2, z: 4, core: 2. Of those that a mesh axis runs over, the one named last changes fastest.
Arguments:
- obs_local: float32 [2, 3, 32768], P(None, None, ('tile', 'pass')), may hold values from -0.2 to 1.2
- obs_value: float32 [32768], P(('tile', 'pass')), may hold values from -6 to 6
- obs_weight: float32 [32768], P(('tile', 'pass')), may hold values from 0.5 to 8
- seg_tiles: int32 [512, 2], P(('tile', 'pass')), may hold values from 0 to 7, all different within a row; in each aligned block of 16 rows (0 to 15, 16 to 31, ...) at most 4 rows name the same one
- comp_scale: int32 [1024], P('tile'), may hold values from 0 to 3
- comp_orient: int32 [1024], P('tile'), may hold values from 0 to 7
- comp_place: int32 [1024], P('tile'), may hold values from 0 to 511
Outputs:
- coefficients: float32 [1024], P('tile')
- grid_field: float32 [8, 4, 1024], P('tile', 'pass')
Inputs may be any that keep to these rules, and one draw needn't show every extreme that they name: `seg_tiles`: each row names 2 different tiles. Among the rows of one device no tile is named by more than 4 rows, a bound that some block reaches.
All inputs are finite; a program needn't handle non-finite values.
Results may differ from a plain program's by a relative error of at most 0.0003.
Values sent between devices are 32-bit elements; how exact they have to be, the bound alone decides.
A program may use at most 64 MiB of HBM per device.

v0:
```python
import math

import jax
import jax.numpy as jnp
from jax import lax
from jax.sharding import PartitionSpec as P

ITERS = 2
GX = 32
GY = 32
DAYS_DEV = 1


TIME_RATE = 8.0
HIGHEST = lax.Precision.HIGHEST


def with_halo(value, sides, width):
    for axis, dim in sides:
        devices, length = (lax.axis_size(axis), value.shape[dim])
        up = [(i, (i + 1) % devices) for i in range(devices)]
        down = [(j, i) for i, j in up]
        last = lax.slice_in_dim(value, length - width, length, axis=dim)
        initial = lax.slice_in_dim(value, 0, width, axis=dim)
        before = lax.ppermute(last, axis, up)
        after = lax.ppermute(initial, axis, down)
        value = jnp.concatenate([before, value, after], axis=dim)
    return value


def wavelet_table(scale_index, orient_index, place_index):
    level = scale_index.astype(jnp.float32)
    width = 0.4 * jnp.power(0.7, level)
    wave_number = 2.2 / width
    angle = math.pi * orient_index.astype(jnp.float32) / 8.0
    center_x = ((place_index % 8).astype(jnp.float32) + 0.5) / 8.0
    center_y = ((place_index // 8 % 8).astype(jnp.float32) + 0.5) / 8.0
    center_t = ((place_index // 64).astype(jnp.float32) + 0.5) / 8.0
    return jnp.stack(
        [
            center_x,
            center_y,
            center_t,
            0.5 / (width * width),
            wave_number * jnp.cos(angle),
            wave_number * jnp.sin(angle),
        ]
    )


def gabor_value(delta_x, delta_y, delta_t, inverse_width, wave_x, wave_y):
    envelope = jnp.exp(
        -(delta_x * delta_x + delta_y * delta_y) * inverse_width - TIME_RATE * delta_t * delta_t
    )
    return envelope * jnp.cos(delta_x * wave_x + delta_y * wave_y)


def slot_basis(slot_block, wavelets):
    delta_x = slot_block[0][:, None] - wavelets[0][None, :]
    delta_y = slot_block[1][:, None] - wavelets[1][None, :]
    delta_t = slot_block[2][:, None] - wavelets[2][None, :]
    return gabor_value(
        delta_x, delta_y, delta_t, wavelets[3][None, :], wavelets[4][None, :], wavelets[5][None, :]
    )


def slot_blocks(slot_points):
    slot_total = slot_points.shape[1]
    block_rows = math.gcd(slot_total, 1024)
    return slot_points.reshape(3, slot_total // block_rows, block_rows).transpose(1, 0, 2)


def tile_forward(slot_points, wavelets, direction):

    def evaluate_block(slot_block):
        return jnp.dot(slot_basis(slot_block, wavelets), direction, precision=HIGHEST)

    return lax.map(evaluate_block, slot_blocks(slot_points)).reshape(-1)


def tile_adjoint(slot_points, wavelets, values):
    blocked = slot_blocks(slot_points)
    value_blocks = values.reshape(blocked.shape[0], -1)

    def accumulate(running, inputs):
        slot_block, value = inputs
        return (running + jnp.dot(value, slot_basis(slot_block, wavelets), precision=HIGHEST), None)

    running, _ = lax.scan(
        accumulate, jnp.zeros((wavelets.shape[1],), jnp.float32), (blocked, value_blocks)
    )
    return running


def pass_total(partial_sums):
    return lax.psum(partial_sums, "pass")


def tile_total(values):
    return lax.psum(jnp.sum(values), "tile")


def on_device(obs_local, obs_value, obs_weight, seg_tiles, comp_scale, comp_orient, comp_place):
    tile_count = lax.axis_size("tile")
    seg_count, fan_out = seg_tiles.shape
    comp_count = comp_scale.shape[0]
    seg_length = obs_value.shape[0] // seg_count
    route_count = seg_count * fan_out
    capacity = max(2, route_count // tile_count)
    wavelets = wavelet_table(comp_scale, comp_orient, comp_place)
    prior_weight = 2.0 * jnp.power(1.5, comp_scale.astype(jnp.float32))
    weights = obs_weight.reshape(seg_count, seg_length)
    weighted_value = weights * obs_value.reshape(seg_count, seg_length)
    positions = (
        obs_local.reshape(fan_out, 3, seg_count, seg_length)
        .transpose(1, 2, 0, 3)
        .reshape(3, route_count, seg_length)
    )
    route_tiles = seg_tiles.reshape(route_count)
    one_hot = (route_tiles[:, None] == jnp.arange(tile_count, dtype=jnp.int32)[None, :]).astype(
        jnp.float32
    )
    slot_rank = jnp.sum((jnp.cumsum(one_hot, axis=0) - one_hot) * one_hot, axis=1).astype(jnp.int32)
    slot_index = route_tiles * capacity + slot_rank
    route_map = (
        slot_index[:, None] == jnp.arange(tile_count * capacity, dtype=jnp.int32)[None, :]
    ).astype(jnp.float32)

    def to_routes(per_point):
        return jnp.broadcast_to(per_point[:, None, :], (seg_count, fan_out, seg_length)).reshape(
            route_count, seg_length
        )

    payload = jnp.concatenate([positions, to_routes(weighted_value)[None]], axis=0)
    outgoing_points = jnp.einsum("fql,qs->fsl", payload, route_map, precision=HIGHEST).reshape(
        4, -1
    )
    arrived = lax.all_to_all(outgoing_points, "tile", split_axis=1, concat_axis=1, tiled=True)
    slot_points = arrived[:3]
    rhs_local = tile_adjoint(slot_points, wavelets, arrived[3])
    rhs = pass_total(rhs_local)
    coefficients = jnp.zeros_like(rhs)
    residual = rhs
    direction = rhs
    norm_now = tile_total(residual * residual)
    for iteration in range(ITERS):
        values = tile_forward(slot_points, wavelets, direction)
        returned = lax.all_to_all(values, "tile", split_axis=0, concat_axis=0, tiled=True)
        at_routes = jnp.dot(
            route_map, returned.reshape(tile_count * capacity, seg_length), precision=HIGHEST
        )
        weighted = weights * jnp.sum(at_routes.reshape(seg_count, fan_out, seg_length), axis=1)
        outgoing = jnp.einsum(
            "qs,ql->sl", route_map, to_routes(weighted), precision=HIGHEST
        ).reshape(-1)
        incoming = lax.all_to_all(outgoing, "tile", split_axis=0, concat_axis=0, tiled=True)
        image = pass_total(tile_adjoint(slot_points, wavelets, incoming)) + prior_weight * direction
        step_size = norm_now / tile_total(direction * image)
        coefficients = coefficients + step_size * direction
        residual = residual - step_size * image
        norm_next = tile_total(residual * residual)
        direction = residual + norm_next / norm_now * direction
        norm_now = norm_next
    stacked = jnp.concatenate([coefficients[None], wavelets], axis=0)
    rim_values = with_halo(stacked, (("tile", 1),), comp_count)
    day_total = DAYS_DEV * lax.axis_size("pass")
    first_day = lax.axis_index("pass") * DAYS_DEV
    day_time = (
        (first_day + jnp.arange(DAYS_DEV, dtype=jnp.int32)).astype(jnp.float32) + 0.5
    ) / day_total
    cell_x = (jnp.arange(GX, dtype=jnp.float32) + 0.5) / GX
    cell_y = (jnp.arange(GY, dtype=jnp.float32) + 0.5) / GY
    place_x = jnp.repeat(cell_x, GY)
    place_y = jnp.tile(cell_y, GX)
    field = jnp.zeros((DAYS_DEV, GX * GY), jnp.float32)
    for neighbor in range(3):
        offset = neighbor - 1
        section = rim_values[:, neighbor * comp_count : (neighbor + 1) * comp_count]
        params = section[1:]
        delta_x = place_x[None, :, None] - (params[0] + offset)[None, None, :]
        delta_y = place_y[None, :, None] - params[1][None, None, :]
        delta_t = day_time[:, None, None] - params[2][None, None, :]
        basis = gabor_value(
            delta_x,
            delta_y,
            delta_t,
            params[3][None, None, :],
            params[4][None, None, :],
            params[5][None, None, :],
        )
        field = field + jnp.einsum("dgk,k->dg", basis, section[0], precision=HIGHEST)
    return (coefficients, field[None])


def solution(mesh):
    return jax.shard_map(
        on_device,
        mesh=mesh,
        in_specs=(
            P(None, None, ("tile", "pass")),
            P(("tile", "pass")),
            P(("tile", "pass")),
            P(("tile", "pass"), None),
            P("tile"),
            P("tile"),
            P("tile"),
        ),
        out_specs=(P("tile"), P("tile", "pass", None)),
        check_vma=False,
    )
```

profile of v0, /device:TPU:0, one launch (start us, length us, event | category | flops | bytes accessed | tf_op | source)
XLA Modules:
  0.0 178.3 jit_solution(1923895358991670544)
XLA Ops:
  0.6 0.8 copy.38
  1.8 0.4 copy-done.2
  2.3 0.6 copy-done.3
  3.4 0.6 copy.40
  4.0 7.3 %all-to-all-start = ((f32[4,8,256]{2,0,1:T(4,128)}), f32[4,8,256]{2,0,1:T(4,128)S(1)}, u32[]{:S(2)}, u32[]{:S(2)}) async-start(f32[4,8,256]{2,0,1:T(4,128)} %copy.40), calls=%async_computation | async-start | bytes 65536 | tf_op jit(solution)/shard_map/all_to_all | solution.py:138
  11.3 0.6 copy-done.1
  12.2 5.7 %all-to-all-done = f32[4,8,256]{2,0,1:T(4,128)S(1)} async-done(((f32[4,8,256]{2,0,1:T(4,128)}), f32[4,8,256]{2,0,1:T(4,128)S(1)}, u32[]{:S(2)}, u32[]{:S(2)}) %all-to-all-start) | async-done | bytes 32800 | tf_op jit(solution)/shard_map/all_to_all | solution.py:138
  18.1 4.9 %while.55 = (s32[]{:T(128)}, f32[128]{0:T(128)S(1)}, f32[2,1024]{1,0:T(2,128)S(1)}, f32[2,3,1024]{2,1,0:T(4,128)S(1)}, f32[1,128]{1,0:T(1,128)S(1)}, /*index=5*/...) while((s32[]{:T(128)}, f32[128]{0:T(128)S(1)}, ...), condition=%wide.region_3.4_spmd.clone, body=%wide.region_2.3_spmd.clone.sunk | while | flops 3539205 | bytes 45239 | solution.py:89
  18.1 2.4 %fusion.232 = f32[128]{0:T(128)S(1)} fusion(f32[128]{0:T(128)S(1)} %bitcast.300, f32[128]{0:T(128)S(1)} %bitcast.313, f32[128]{0:T(128)S(1)} %bitcast.307, f32[1024]{0:T(1024)S(1)} %bitcast.256, f32[128]{0:T(128)S(1)} %bitcast.293, f32[128]{0:T(128)S(1)} %bitcast.286, f32[1024]{0:T(1024)S(1)} %bitcast.255, f32[128]{0:T(128)S(1)} %bitcast.279, ...), kind=kOutput, calls=%fused_computation.59.clone.1 | convolution fusion | flops 3539200 | bytes 20485 | tf_op jit(solution)/shard_map/while/body/eval_jaxpr/dot_general | solution.py:87
  20.6 2.4 %fusion.232 = f32[128]{0:T(128)S(1)} fusion(f32[128]{0:T(128)S(1)} %bitcast.300, f32[128]{0:T(128)S(1)} %bitcast.313, f32[128]{0:T(128)S(1)} %bitcast.307, f32[1024]{0:T(1024)S(1)} %bitcast.256, f32[128]{0:T(128)S(1)} %bitcast.293, f32[128]{0:T(128)S(1)} %bitcast.286, f32[1024]{0:T(1024)S(1)} %bitcast.255, f32[128]{0:T(128)S(1)} %bitcast.279, ...), kind=kOutput, calls=%fused_computation.59.clone.1 | convolution fusion | flops 3539200 | bytes 20485 | tf_op jit(solution)/shard_map/while/body/eval_jaxpr/dot_general | solution.py:87
  23.0 5.7 %psum.49 = f32[128]{0:T(128)S(1)} all-reduce(f32[128]{0:T(128)S(1)} %get-tuple-element.262), channel_id=1, replica_groups=mesh['tile'=8,'pass'=4] {'pass'}, use_global_device_ids=true, to_apply=%region_4.5 | all-reduce | flops 128 | bytes 1024 | tf_op jit(solution)/shard_map/psum | solution.py:96
  28.7 5.9 %while.53 = (s32[]{:T(128)}, f32[2,1024]{1,0:T(2,128)S(1)}, f32[2,3,1024]{2,1,0:T(4,128)S(1)}, f32[1,128]{1,0:T(1,128)S(1)}, f32[1,128]{1,0:T(1,128)S(1)}, /*ind...) while((s32[]{:T(128)}, f32[2,1024]{1,0:T(2,128)S(1)}, ...), condition=%wide.region_8.9_spmd, body=%wide.region_7.8_spmd.sunk | while | flops 3538948 | bytes 52909 | solution.py:78
  28.7 2.8 %fusion.226 = f32[1,1024]{1,0:T(1,128)S(1)} fusion(f32[128]{0:T(128)S(1)} %bitcast.301, f32[128]{0:T(128)S(1)} %bitcast.314, f32[128]{0:T(128)S(1)} %bitcast.308, f32[1024]{0:T(1024)S(1)} %bitcast.265, f32[128]{0:T(128)S(1)} %bitcast.294, f32[128]{0:T(128)S(1)} %bitcast.287, f32[1024]{0:T(1024)S(1)} %bitcast.264, f32[128]{0:T(128)S(1)} %bitcast.280, ...), kind=kOutput, calls=%fused_computation.13.clone.1 | convolution fusion | flops 3538944 | bytes 19968 | tf_op jit(solution)/shard_map/while/body/eval_jaxpr/dot_general | solution.py:76
  31.6 2.8 %fusion.226 = f32[1,1024]{1,0:T(1,128)S(1)} fusion(f32[128]{0:T(128)S(1)} %bitcast.301, f32[128]{0:T(128)S(1)} %bitcast.314, f32[128]{0:T(128)S(1)} %bitcast.308, f32[1024]{0:T(1024)S(1)} %bitcast.265, f32[128]{0:T(128)S(1)} %bitcast.294, f32[128]{0:T(128)S(1)} %bitcast.287, f32[1024]{0:T(1024)S(1)} %bitcast.264, f32[128]{0:T(128)S(1)} %bitcast.280, ...), kind=kOutput, calls=%fused_computation.13.clone.1 | convolution fusion | flops 3538944 | bytes 19968 | tf_op jit(solution)/shard_map/while/body/eval_jaxpr/dot_general | solution.py:76
  34.6 0.6 all_to_all.32
  35.2 3.5 %all-to-all-start.1 = ((f32[8,256,1]{1,2,0:T(1,128)}), f32[8,256,1]{1,2,0:T(1,128)S(1)}, u32[]{:S(2)}, u32[]{:S(2)}) async-start(f32[8,256,1]{1,2,0:T(1,128)} %all_to_all.32), calls=%async_computation.1 | async-start | bytes 16384 | tf_op jit(solution)/shard_map/all_to_all | solution.py:148
  38.7 6.4 %all-to-all-done.1 = f32[8,256,1]{1,2,0:T(1,128)S(1)} async-done(((f32[8,256,1]{1,2,0:T(1,128)}), f32[8,256,1]{1,2,0:T(1,128)S(1)}, u32[]{:S(2)}, u32[]{:S(2)}) %all-to-all-start.1) | async-done | bytes 8224 | tf_op jit(solution)/shard_map/all_to_all | solution.py:148
  45.2 0.2 convolution_reduce_fusion.1
  45.5 0.7 all_to_all.40
  46.2 3.3 %all-to-all-start.2 = ((f32[8,256,1]{1,2,0:T(1,128)}), f32[8,256,1]{1,2,0:T(1,128)S(1)}, u32[]{:S(2)}, u32[]{:S(2)}) async-start(f32[8,256,1]{1,2,0:T(1,128)} %all_to_all.40), calls=%async_computation.2 | async-start | bytes 16384 | tf_op jit(solution)/shard_map/all_to_all | solution.py:156
  49.6 6.4 %all-to-all-done.2 = f32[8,256,1]{1,2,0:T(1,128)S(1)} async-done(((f32[8,256,1]{1,2,0:T(1,128)}), f32[8,256,1]{1,2,0:T(1,128)S(1)}, u32[]{:S(2)}, u32[]{:S(2)}) %all-to-all-start.2) | async-done | bytes 8224 | tf_op jit(solution)/shard_map/all_to_all | solution.py:156
  56.1 4.9 %while.56 = (s32[]{:T(128)}, f32[128]{0:T(128)S(1)}, f32[2,1024]{1,0:T(2,128)S(1)}, f32[2,3,1024]{2,1,0:T(4,128)S(1)}, f32[1,128]{1,0:T(1,128)S(1)}, /*index=5*/...) while((s32[]{:T(128)}, f32[128]{0:T(128)S(1)}, ...), condition=%wide.region_11.12_spmd.clone, body=%wide.region_10.11_spmd.clone.sunk | while | flops 3539205 | bytes 45239 | solution.py:89
  56.1 2.4 %fusion.235 = f32[128]{0:T(128)S(1)} fusion(f32[128]{0:T(128)S(1)} %bitcast.302, f32[128]{0:T(128)S(1)} %bitcast.315, f32[128]{0:T(128)S(1)} %bitcast.309, f32[1024]{0:T(1024)S(1)} %bitcast.259, f32[128]{0:T(128)S(1)} %bitcast.295, f32[128]{0:T(128)S(1)} %bitcast.288, f32[1024]{0:T(1024)S(1)} %bitcast.258, f32[128]{0:T(128)S(1)} %bitcast.281, ...), kind=kOutput, calls=%fused_computation.93.clone.1 | convolution fusion | flops 3539200 | bytes 20485 | tf_op jit(solution)/shard_map/while/body/eval_jaxpr/dot_general | solution.py:87
  58.6 2.4 %fusion.235 = f32[128]{0:T(128)S(1)} fusion(f32[128]{0:T(128)S(1)} %bitcast.302, f32[128]{0:T(128)S(1)} %bitcast.315, f32[128]{0:T(128)S(1)} %bitcast.309, f32[1024]{0:T(1024)S(1)} %bitcast.259, f32[128]{0:T(128)S(1)} %bitcast.295, f32[128]{0:T(128)S(1)} %bitcast.288, f32[1024]{0:T(1024)S(1)} %bitcast.258, f32[128]{0:T(128)S(1)} %bitcast.281, ...), kind=kOutput, calls=%fused_computation.93.clone.1 | convolution fusion | flops 3539200 | bytes 20485 | tf_op jit(solution)/shard_map/while/body/eval_jaxpr/dot_general | solution.py:87
  61.0 5.7 %psum.51 = f32[128]{0:T(128)S(1)} all-reduce(f32[128]{0:T(128)S(1)} %get-tuple-element.264), channel_id=1, replica_groups=mesh['tile'=8,'pass'=4] {'pass'}, use_global_device_ids=true, to_apply=%region_12.13 | all-reduce | flops 128 | bytes 1024 | tf_op jit(solution)/shard_map/psum | solution.py:96
  66.7 0.6 multiply_reduce_fusion.2
  67.3 18.3 %all-reduce = (f32[]{:T(128)}, f32[]{:T(128)}) all-reduce(f32[]{:T(128)} %get-tuple-element.517, f32[]{:T(128)} %get-tuple-element.516), channel_id=1, replica_groups=mesh['tile'=8,'pass'=4] {'tile'}, use_global_device_ids=true, to_apply=%region_6.7 | all-reduce | flops 2 | bytes 16 | tf_op jit(solution)/shard_map/psum | solution.py:100
  86.9 0.6 multiply_reduce_fusion.1
  87.5 19.2 %psum.53 = f32[]{:T(128)} all-reduce(f32[]{:T(128)} %multiply_reduce_fusion.1), channel_id=1, replica_groups=mesh['tile'=8,'pass'=4] {'tile'}, use_global_device_ids=true, to_apply=%region_16.17 | all-reduce | flops 1 | bytes 8 | tf_op jit(solution)/shard_map/psum | solution.py:100
  108.0 5.9 %while.54 = (s32[]{:T(128)}, f32[2,1024]{1,0:T(2,128)S(1)}, f32[2,3,1024]{2,1,0:T(4,128)S(1)}, f32[1,128]{1,0:T(1,128)S(1)}, f32[1,128]{1,0:T(1,128)S(1)}, /*ind...) while((s32[]{:T(128)}, f32[2,1024]{1,0:T(2,128)S(1)}, ...), condition=%wide.region_18.19_spmd, body=%wide.region_17.18_spmd.sunk | while | flops 3538948 | bytes 52909 | solution.py:78
  108.0 2.8 %fusion.229 = f32[1,1024]{1,0:T(1,128)S(1)} fusion(f32[128]{0:T(128)S(1)} %bitcast.303, f32[128]{0:T(128)S(1)} %bitcast.316, f32[128]{0:T(128)S(1)} %bitcast.310, f32[1024]{0:T(1024)S(1)} %bitcast.268, f32[128]{0:T(128)S(1)} %bitcast.296, f32[128]{0:T(128)S(1)} %bitcast.289, f32[1024]{0:T(1024)S(1)} %bitcast.267, f32[128]{0:T(128)S(1)} %bitcast.282, ...), kind=kOutput, calls=%fused_computation.42.clone.1 | convolution fusion | flops 3538944 | bytes 19968 | tf_op jit(solution)/shard_map/while/body/eval_jaxpr/dot_general | solution.py:76
  111.0 2.8 %fusion.229 = f32[1,1024]{1,0:T(1,128)S(1)} fusion(f32[128]{0:T(128)S(1)} %bitcast.303, f32[128]{0:T(128)S(1)} %bitcast.316, f32[128]{0:T(128)S(1)} %bitcast.310, f32[1024]{0:T(1024)S(1)} %bitcast.268, f32[128]{0:T(128)S(1)} %bitcast.296, f32[128]{0:T(128)S(1)} %bitcast.289, f32[1024]{0:T(1024)S(1)} %bitcast.267, f32[128]{0:T(128)S(1)} %bitcast.282, ...), kind=kOutput, calls=%fused_computation.42.clone.1 | convolution fusion | flops 3538944 | bytes 19968 | tf_op jit(solution)/shard_map/while/body/eval_jaxpr/dot_general | solution.py:76
  113.9 8.9 %all_to_all.47 = f32[8,256,1]{1,2,0:T(1,128)S(1)} all-to-all(f32[8,256,1]{1,2,0:T(1,128)S(1)} %all_to_all.36), channel_id=1, replica_groups=mesh['tile'=8,'pass'=4] {'tile'}, dimensions={0} | all-to-all | bytes 16384 | tf_op jit(solution)/shard_map/all_to_all | solution.py:148
  123.3 0.7 all_to_all.41
  123.9 3.5 %all-to-all-start.4 = ((f32[8,256,1]{1,2,0:T(1,128)}), f32[8,256,1]{1,2,0:T(1,128)S(1)}, u32[]{:S(2)}, u32[]{:S(2)}) async-start(f32[8,256,1]{1,2,0:T(1,128)} %all_to_all.41), calls=%async_computation.4 | async-start | bytes 16384 | tf_op jit(solution)/shard_map/all_to_all | solution.py:156
  127.6 6.1 %all-to-all-done.4 = f32[8,256,1]{1,2,0:T(1,128)S(1)} async-done(((f32[8,256,1]{1,2,0:T(1,128)}), f32[8,256,1]{1,2,0:T(1,128)S(1)}, u32[]{:S(2)}, u32[]{:S(2)}) %all-to-all-start.4) | async-done | bytes 8224 | tf_op jit(solution)/shard_map/all_to_all | solution.py:156
  133.8 4.9 %while.57 = (s32[]{:T(128)}, f32[128]{0:T(128)S(1)}, f32[2,1024]{1,0:T(2,128)S(1)}, f32[2,3,1024]{2,1,0:T(4,128)S(1)}, f32[1,128]{1,0:T(1,128)S(1)}, /*index=5*/...) while((s32[]{:T(128)}, f32[128]{0:T(128)S(1)}, ...), condition=%wide.region_21.22_spmd.clone, body=%wide.region_20.21_spmd.clone.sunk | while | flops 3539205 | bytes 45239 | solution.py:89
  133.8 2.4 %fusion.238 = f32[128]{0:T(128)S(1)} fusion(f32[128]{0:T(128)S(1)} %bitcast.304, f32[128]{0:T(128)S(1)} %bitcast.317, f32[128]{0:T(128)S(1)} %bitcast.311, f32[1024]{0:T(1024)S(1)} %bitcast.262, f32[128]{0:T(128)S(1)} %bitcast.297, f32[128]{0:T(128)S(1)} %bitcast.290, f32[1024]{0:T(1024)S(1)} %bitcast.261, f32[128]{0:T(128)S(1)} %bitcast.283, ...), kind=kOutput, calls=%fused_computation.127.clone.1 | convolution fusion | flops 3539200 | bytes 20485 | tf_op jit(solution)/shard_map/while/body/eval_jaxpr/dot_general | solution.py:87
  136.3 2.4 %fusion.238 = f32[128]{0:T(128)S(1)} fusion(f32[128]{0:T(128)S(1)} %bitcast.304, f32[128]{0:T(128)S(1)} %bitcast.317, f32[128]{0:T(128)S(1)} %bitcast.311, f32[1024]{0:T(1024)S(1)} %bitcast.262, f32[128]{0:T(128)S(1)} %bitcast.297, f32[128]{0:T(128)S(1)} %bitcast.290, f32[1024]{0:T(1024)S(1)} %bitcast.261, f32[128]{0:T(128)S(1)} %bitcast.283, ...), kind=kOutput, calls=%fused_computation.127.clone.1 | convolution fusion | flops 3539200 | bytes 20485 | tf_op jit(solution)/shard_map/while/body/eval_jaxpr/dot_general | solution.py:87
  138.7 5.7 %psum.54 = f32[128]{0:T(128)S(1)} all-reduce(f32[128]{0:T(128)S(1)} %get-tuple-element.266), channel_id=1, replica_groups=mesh['tile'=8,'pass'=4] {'pass'}, use_global_device_ids=true, to_apply=%region_22.23 | all-reduce | flops 128 | bytes 1024 | tf_op jit(solution)/shard_map/psum | solution.py:96
  144.4 0.6 multiply_reduce_fusion
  145.1 18.3 %psum.55 = f32[]{:T(128)} all-reduce(f32[]{:T(128)} %multiply_reduce_fusion), channel_id=1, replica_groups=mesh['tile'=8,'pass'=4] {'tile'}, use_global_device_ids=true, to_apply=%region_24.25 | all-reduce | flops 1 | bytes 8 | tf_op jit(solution)/shard_map/psum | solution.py:100
  164.6 1.5 collective-permute-start
  166.2 3.2 %collective-permute-start.1 = (f32[7,128]{1,0:T(8,128)S(1)}, f32[7,128]{1,0:T(8,128)S(1)}, u32[]{:S(2)}, u32[]{:S(2)}) collective-permute-start(f32[7,128]{1,0:T(8,128)S(1)} %concatenate.7), channel_id=1, source_target_pairs={{4,0},{8,4},{12,8},{16,12},{20,16},{24,20},{28,24},{0,28},{5,1},{9... | collective-permute-start | bytes 10760 | tf_op jit(solution)/shard_map/ppermute | solution.py:26
  169.4 2.7 %fusion.148 = f32[1,1024]{1,0:T(1,128)S(1)} fusion(f32[128]{0:T(128)S(1)} %bitcast.305, f32[128]{0:T(128)S(1)} %bitcast.318, f32[128]{0:T(128)S(1)} %get-tuple-element.620, f32[128]{0:T(128)S(1)} %bitcast.298, f32[128]{0:T(128)S(1)} %bitcast.291, f32[128]{0:T(128)S(1)} %bitcast.284, f32[1024]{0:T(1024)S(1)} %sub.484, f32[1024]{0:T(1024)S(1)} %sub.480, ...), kind=kOutput, calls=%fused_computation.200 | convolution fusion | flops 3145728 | bytes 15872 | tf_op jit(solution)/shard_map/dgk,k->dg/dot_general | solution.py:191
  172.2 2.7 %fusion.150 = f32[1,1024]{1,0:T(1,128)S(1)} fusion(f32[128]{0:T(128)S(1)} %get-tuple-element.640, f32[128]{0:T(128)S(1)} %get-tuple-element.641, f32[128]{0:T(128)S(1)} %multiply_multiply_fusion.10, f32[128]{0:T(128)S(1)} %get-tuple-element.642, f32[128]{0:T(128)S(1)} %get-tuple-element.643, f32[1024]{0:T(1024)S(1)} %sub.484, ...), kind=kOutput, calls=%fused_computation.201 | convolution fusion | flops 3145728 | bytes 15872 | tf_op jit(solution)/shard_map/dgk,k->dg/dot_general | solution.py:191
  175.0 2.7 %fusion.146 = f32[1,1024]{1,0:T(1,128)S(1)} fusion(f32[128]{0:T(128)S(1)} %get-tuple-element.645, f32[128]{0:T(128)S(1)} %get-tuple-element.646, f32[128]{0:T(128)S(1)} %multiply_multiply_fusion.8, f32[128]{0:T(128)S(1)} %get-tuple-element.647, f32[128]{0:T(128)S(1)} %get-tuple-element.648, f32[128]{0:T(128)S(1)} %get-tuple-element.644, ...), kind=kOutput, calls=%fused_computation.199 | convolution fusion | flops 3145728 | bytes 15872 | tf_op jit(solution)/shard_map/dgk,k->dg/dot_general | solution.py:191
  177.7 0.6 add_add_fusion
  (86 shorter events, 2.8 us)
Async XLA Ops:
  1.5 0.7 copy-start.2
  1.6 1.4 copy-start
  2.2 0.7 copy-start.3
  4.0 13.9 %all-to-all-start = ((f32[4,8,256]{2,0,1:T(4,128)}), f32[4,8,256]{2,0,1:T(4,128)S(1)}, u32[]{:S(2)}, u32[]{:S(2)}) async-start(f32[4,8,256]{2,0,1:T(4,128)} %copy.40), calls=%async_computation | async-start | bytes 65536 | tf_op jit(solution)/shard_map/all_to_all | solution.py:138
  11.3 0.7 copy-start.1
  11.3 0.7 copy-start.6
  11.3 0.7 copy-start.7
  35.2 3.5 %copy-start.4 = (s32[16,2]{0,1:T(2,128)S(1)}, s32[16,2]{0,1:T(2,128)}, u32[]{:S(2)}) copy-start(s32[16,2]{0,1:T(2,128)} %param.20) | copy-start | bytes 388
  35.2 9.9 %all-to-all-start.1 = ((f32[8,256,1]{1,2,0:T(1,128)}), f32[8,256,1]{1,2,0:T(1,128)S(1)}, u32[]{:S(2)}, u32[]{:S(2)}) async-start(f32[8,256,1]{1,2,0:T(1,128)} %all_to_all.32), calls=%async_computation.1 | async-start | bytes 16384 | tf_op jit(solution)/shard_map/all_to_all | solution.py:148
  46.2 9.8 %all-to-all-start.2 = ((f32[8,256,1]{1,2,0:T(1,128)}), f32[8,256,1]{1,2,0:T(1,128)S(1)}, u32[]{:S(2)}, u32[]{:S(2)}) async-start(f32[8,256,1]{1,2,0:T(1,128)} %all_to_all.40), calls=%async_computation.2 | async-start | bytes 16384 | tf_op jit(solution)/shard_map/all_to_all | solution.py:156
  123.9 9.8 %all-to-all-start.4 = ((f32[8,256,1]{1,2,0:T(1,128)}), f32[8,256,1]{1,2,0:T(1,128)S(1)}, u32[]{:S(2)}, u32[]{:S(2)}) async-start(f32[8,256,1]{1,2,0:T(1,128)} %all_to_all.41), calls=%async_computation.4 | async-start | bytes 16384 | tf_op jit(solution)/shard_map/all_to_all | solution.py:156
  164.6 4.8 %copy-start.5 = (f32[128]{0:T(128)}, f32[128]{0:T(128)S(1)}, u32[]{:S(2)}) copy-start(f32[128]{0:T(128)S(1)} %multiply_add_fusion.1) | copy-start | bytes 1540
  164.6 7.5 %collective-permute-start = (f32[7,128]{1,0:T(8,128)S(1)}, f32[7,128]{1,0:T(8,128)S(1)}, u32[]{:S(2)}, u32[]{:S(2)}) collective-permute-start(f32[7,128]{1,0:T(8,128)S(1)} %concatenate.7), channel_id=1, source_target_pairs={{0,4},{4,8},{8,12},{12,16},{16,20},{20,24},{24,28},{28,0},{1,5},{5... | collective-permute-start | bytes 10760 | tf_op jit(solution)/shard_map/ppermute | solution.py:25
  166.2 6.0 %collective-permute-start.1 = (f32[7,128]{1,0:T(8,128)S(1)}, f32[7,128]{1,0:T(8,128)S(1)}, u32[]{:S(2)}, u32[]{:S(2)}) collective-permute-start(f32[7,128]{1,0:T(8,128)S(1)} %concatenate.7), channel_id=1, source_target_pairs={{4,0},{8,4},{12,8},{16,12},{20,16},{24,20},{28,24},{0,28},{5,1},{9... | collective-permute-start | bytes 10760 | tf_op jit(solution)/shard_map/ppermute | solution.py:26
where the time goes:
time: 179 us; the launch traced here: 178 us
  blocking collectives  81.7 us (46%)
  matrix products  34.8 us (19%)
  waiting for transfers between devices  24.7 us (14%)
  starting transfers between devices  22.3 us (12%)
  local copies, waits for them, and re-layouts  6.67 us (4%)
  between operations  4.83 us (3%)
  other arithmetic  3.07 us (2%)
    psum x3, blocking collectives, tile_total(): return lax.psum(jnp.sum(values), 'tile')  55.8 us
    psum x3, blocking collectives, pass_total(): return lax.psum(partial_sums, 'pass')  17 us
    dot_general x6, matrix products, accumulate(): jnp.dot(value, slot_basis(slot_block, wavelets), precision=HIGHEST)  14.4 us
    all_to_all x2, waiting for transfers between devices, on_device(): lax.all_to_all(outgoing, 'tile', split_axis=0, concat_axis=0, tiled=True)  12.5 us
    dot_general x4, matrix products, evaluate_block(): jnp.dot(slot_basis(slot_block, wavelets), direction, precision=HIGHEST)  11.4 us
    all_to_all x1, blocking collectives, on_device(): lax.all_to_all(values, 'tile', split_axis=0, concat_axis=0, tiled=True)  8.88 us
    dot_general x3, matrix products, on_device(): jnp.einsum('dgk,k->dg', basis, section[0], precision=HIGHEST)  8.18 us
    all_to_all x1, starting transfers between devices, on_device(): lax.all_to_all(outgoing_points, 'tile', split_axis=1, concat_axis=1, tile...  7.25 us
  transfers between devices with their start and end apart: 6, of which 4 were waited for; matrix products, arithmetic and copies ran while one was open for 2% of the time, Pallas kernels for 0%

commit v1 on v0

v1 whole, which is shorter than its diff:
```python
import functools
import math

import jax
import jax.numpy as jnp
import numpy as np
from jax import lax
from jax.experimental import pallas as pl
from jax.experimental.pallas import tpu as pltpu
from jax.sharding import PartitionSpec as P

GX = 32
GY = 32
LANES = 128
TIME_RATE = 8.0
LOG2E = math.log2(math.e)
TIME_SCALE = math.sqrt(TIME_RATE * LOG2E)
ROUNDER = 12582912.0
HIGHEST = lax.Precision.HIGHEST
MESH = pl.DeviceIdType.MESH


def cosine_polynomial(degree):
    fit = np.polynomial.Chebyshev.interpolate(
        lambda z: np.cos(2 * np.pi * np.sqrt(np.maximum(z, 0.0))), degree, domain=[0.0, 0.25]
    )
    return [float(c) for c in fit.convert(kind=np.polynomial.Polynomial).coef]


COSINE = cosine_polynomial(6)


def cos_turns(turns):
    part = turns - jnp.round(turns)
    square = part * part
    total = jnp.full_like(square, COSINE[-1])
    for coefficient in COSINE[-2::-1]:
        total = total * square + coefficient
    return total


def peers(count, body):
    if count <= 8:
        for distance in range(1, count):
            body(distance)
    else:

        def step(distance, carry):
            body(distance)
            return carry

        lax.fori_loop(1, count, step, 0)


def total_of(value):
    return jnp.sum(jnp.sum(value, axis=1, keepdims=True), axis=0, keepdims=True)


def kernel(
    tiles, passes, obs_ref, value_ref, weight_ref, seg_ref, scale_ref, orient_ref, place_ref,
    coef_ref, field_ref,
    table, stack, columns, basis, vectors, grid_x, grid_y,
    near, far, last_near, last_far, table_sems, near_sems, far_sems,
):
    my_tile, my_pass = lax.axis_index("tile"), lax.axis_index("pass")
    seg_count, fan_out = seg_ref.shape
    points = value_ref.shape[1]
    seg_length = points // seg_count

    barrier = pltpu.get_barrier_semaphore()
    peers(passes, lambda d: pl.semaphore_signal(
        barrier, inc=1, device_id={"pass": lax.rem(my_pass + d, passes)}, device_id_type=MESH))
    peers(tiles, lambda d: pl.semaphore_signal(
        barrier, inc=1, device_id={"tile": lax.rem(my_tile + d, tiles)}, device_id_type=MESH))

    def to_peer(buffer, axis, me, count, sems, distance):
        return pltpu.make_async_remote_copy(
            src_ref=buffer.at[me],
            dst_ref=buffer.at[me],
            send_sem=sems.at[0, distance],
            recv_sem=sems.at[1, distance],
            device_id={axis: lax.rem(me + distance, count)},
            device_id_type=MESH,
        )

    level = scale_ref[...].astype(jnp.float32)
    width = 0.4 * jnp.exp(level * math.log(0.7))
    wave = 2.2 / (2.0 * math.pi) / width
    turns = orient_ref[...].astype(jnp.float32) / 16.0
    place = place_ref[...]
    table[my_tile, 0:1, :] = ((place & 7).astype(jnp.float32) + 0.5) / 8.0
    table[my_tile, 1:2, :] = (((place >> 3) & 7).astype(jnp.float32) + 0.5) / 8.0
    table[my_tile, 2:3, :] = ((place >> 6).astype(jnp.float32) + 0.5) * (TIME_SCALE / 8.0)
    table[my_tile, 3:4, :] = 0.5 * LOG2E / (width * width)
    table[my_tile, 4:5, :] = wave * cos_turns(turns)
    table[my_tile, 5:6, :] = wave * cos_turns(turns - 0.25)
    table[my_tile, 6:7, :] = 2.0 * jnp.exp(level * math.log(1.5))
    table[my_tile, 7:8, :] = jnp.zeros((1, LANES), jnp.float32)

    pl.semaphore_wait(barrier, passes + tiles - 2)
    peers(tiles, lambda d: to_peer(table, "tile", my_tile, tiles, table_sems, d).start())

    weights = weight_ref[...]
    for route in range(fan_out):
        stack[3 * route : 3 * route + 2, :] = obs_ref[route, 0:2, :]
        stack[3 * route + 2 : 3 * route + 3, :] = obs_ref[route, 2:3, :] * TIME_SCALE
    stack[3 * fan_out : 3 * fan_out + 1, :] = weights
    stack[3 * fan_out + 1 : 3 * fan_out + 2, :] = weights * value_ref[...]
    for start in range(0, points, LANES):
        columns[start : start + LANES, :] = stack[:, start : start + LANES].T

    def column(seg, which):
        rows = pl.ds(pl.multiple_of(seg * seg_length, seg_length), seg_length)
        return jnp.broadcast_to(columns[rows, which : which + 1], (seg_length, LANES))

    peers(tiles, lambda d: to_peer(table, "tile", my_tile, tiles, table_sems, d).wait_recv())

    tile_row = lax.broadcasted_iota(jnp.int32, (tiles, LANES), 0)

    def gather_into(running, tile, block):
        part = jnp.sum(block, axis=0, keepdims=True)
        return running + jnp.where(tile_row == tile, part, 0.0)

    def build(seg, running):
        weighted = column(seg, 3 * fan_out + 1)
        for route in range(fan_out):
            tile = seg_ref[seg, route]
            param = lambda row: table[tile, row : row + 1, :]
            delta_x = column(seg, 3 * route) - param(0)
            delta_y = column(seg, 3 * route + 1) - param(1)
            delta_t = column(seg, 3 * route + 2) - param(2)
            envelope = jnp.exp2(
                -(delta_x * delta_x + delta_y * delta_y) * param(3) - delta_t * delta_t
            )
            phi = envelope * cos_turns(delta_x * param(4) + delta_y * param(5))
            basis[seg * fan_out + route] = phi
            running = gather_into(running, tile, phi * weighted)
        return running

    def forward(which, seg):
        total = jnp.zeros((seg_length, LANES), jnp.float32)
        for route in range(fan_out):
            tile = seg_ref[seg, route]
            total = total + basis[seg * fan_out + route] * vectors[which, pl.ds(tile, 1), :]
        return jnp.sum(total, axis=1, keepdims=True)

    def normal(seg, running):
        weighted = forward(0, seg) * column(seg, 3 * fan_out)
        for route in range(fan_out):
            running = gather_into(
                running, seg_ref[seg, route], basis[seg * fan_out + route] * weighted
            )
        return running

    def energy(seg, running):
        values = forward(1, seg)
        return running + values * values * column(seg, 3 * fan_out)

    def sum_slots(buffer, count):
        if count <= 8:
            total = buffer[0]
            for slot in range(1, count):
                total = total + buffer[slot]
            return total
        return lax.fori_loop(1, count, lambda slot, total: total + buffer[slot], buffer[0])

    def all_sum(value, near_slots, far_slots, near_sem, far_sem, beside=None):
        near_slots[my_pass] = value
        peers(passes, lambda d: to_peer(near_slots, "pass", my_pass, passes, near_sem, d).start())
        if beside is not None:
            beside[0]()
        peers(passes, lambda d: to_peer(near_slots, "pass", my_pass, passes, near_sem, d).wait_recv())
        far_slots[my_tile] = sum_slots(near_slots, passes)
        peers(tiles, lambda d: to_peer(far_slots, "tile", my_tile, tiles, far_sem, d).start())
        if beside is not None:
            beside[1]()
        peers(tiles, lambda d: to_peer(far_slots, "tile", my_tile, tiles, far_sem, d).wait_recv())
        return sum_slots(far_slots, tiles)

    def grid_params(neighbor):
        tile = lax.rem(my_tile + (neighbor - 1) + tiles, tiles)
        return tile, lambda row: table[tile, row : row + 1, :]

    def axis_factors(delta, inverse, wave_row):
        envelope = jnp.exp2(-(delta * delta) * inverse)
        phase = delta * wave_row
        return envelope * cos_turns(phase), envelope * cos_turns(phase - 0.25)

    def grid_factors_y():
        cell = lax.broadcasted_iota(jnp.int32, (LANES, LANES), 0) & (GY - 1)
        place_y = (cell.astype(jnp.float32) + 0.5) / GY
        for neighbor in range(3):
            _, param = grid_params(neighbor)
            even, odd = axis_factors(place_y - param(1), param(3), param(5))
            grid_y[neighbor, :, :LANES] = even
            grid_y[neighbor, :, LANES:] = odd

    def grid_factors_x():
        row = lax.broadcasted_iota(jnp.int32, (GX, LANES), 0)
        cell = (row & 7) * (GX // 8) + (row >> 3)
        place_x = (cell.astype(jnp.float32) + 0.5) / GX
        day = (my_pass.astype(jnp.float32) + 0.5) / passes * TIME_SCALE
        for neighbor in range(3):
            _, param = grid_params(neighbor)
            even, odd = axis_factors(
                place_x - (param(0) + float(neighbor - 1)), param(3), param(4)
            )
            delta_t = day - param(2)
            in_time = jnp.exp2(-(delta_t * delta_t))
            grid_x[neighbor, :, :LANES] = even * in_time
            grid_x[neighbor, :, LANES:] = -odd * in_time

    zeros = jnp.zeros((tiles, LANES), jnp.float32)
    rhs = all_sum(
        lax.fori_loop(0, seg_count, build, zeros),
        near.at[0], far.at[0], near_sems.at[0], far_sems.at[0],
        (grid_factors_x, grid_factors_y),
    )
    norm_first = total_of(rhs * rhs)
    prior = table[:, 6, :]
    vectors[0] = rhs
    image = all_sum(
        lax.fori_loop(0, seg_count, normal, zeros),
        near.at[1], far.at[1], near_sems.at[1], far_sems.at[1],
    ) + prior * rhs
    step_first = norm_first / total_of(rhs * image)
    residual = rhs - step_first * image
    norm_next = total_of(residual * residual)
    direction = residual + norm_next / norm_first * rhs
    vectors[1] = direction

    fields = []

    def grid_fields():
        total = None
        for neighbor in range(3):
            tile, _ = grid_params(neighbor)
            parts = []
            for which in range(2):
                row = vectors[which, pl.ds(tile, 1), :]
                parts.append(grid_x[neighbor] * jnp.concatenate([row, row], axis=1))
            term = lax.dot_general(
                jnp.concatenate(parts, axis=0),
                grid_y[neighbor],
                (((1,), (1,)), ((), ())),
                precision=HIGHEST,
                preferred_element_type=jnp.float32,
            )
            total = term if total is None else total + term
        group = lax.broadcasted_iota(jnp.int32, (8, LANES), 1) // GY
        for begin in (0, GX):
            field = jnp.zeros((8, LANES), jnp.float32)
            for part in range(GX // 8):
                field = field + jnp.where(
                    group == part, total[begin + 8 * part : begin + 8 * part + 8, :], 0.0
                )
            fields.append(field)

    energies = lax.fori_loop(
        0, seg_count, energy, jnp.zeros((seg_length, LANES), jnp.float32)
    )
    folded = jnp.sum(energies, axis=0, keepdims=True)
    product = all_sum(
        folded, last_near, last_far, near_sems.at[2], far_sems.at[2],
        (grid_fields, lambda: None),
    )[:, 0:1] + total_of(direction * direction * prior)
    step_second = norm_next / product
    mine = pl.ds(my_tile, 1)
    coef_ref[...] = step_first * vectors[0, mine, :] + step_second * vectors[1, mine, :]
    field_ref[...] = step_first * fields[0] + step_second * fields[1]

    peers(tiles, lambda d: to_peer(table, "tile", my_tile, tiles, table_sems, d).wait_send())
    for stage in range(3):
        near_slots = near.at[stage] if stage < 2 else last_near
        far_slots = far.at[stage] if stage < 2 else last_far
        peers(passes, lambda d: to_peer(
            near_slots, "pass", my_pass, passes, near_sems.at[stage], d).wait_send())
        peers(tiles, lambda d: to_peer(
            far_slots, "tile", my_tile, tiles, far_sems.at[stage], d).wait_send())


def on_device(tiles, passes, obs_local, obs_value, obs_weight, seg_tiles, comp_scale, comp_orient, comp_place):
    seg_count, fan_out = seg_tiles.shape
    points = obs_value.shape[0]
    seg_length = points // seg_count
    vmem = pl.BlockSpec(memory_space=pltpu.VMEM)
    coefficients, field = pl.pallas_call(
        functools.partial(kernel, tiles, passes),
        out_shape=(
            jax.ShapeDtypeStruct((1, LANES), jnp.float32),
            jax.ShapeDtypeStruct((8, LANES), jnp.float32),
        ),
        in_specs=[vmem, vmem, vmem, pl.BlockSpec(memory_space=pltpu.SMEM), vmem, vmem, vmem],
        out_specs=(vmem, vmem),
        scratch_shapes=[
            pltpu.VMEM((tiles, 8, LANES), jnp.float32),
            pltpu.VMEM((8, points), jnp.float32),
            pltpu.VMEM((points, 8), jnp.float32),
            pltpu.VMEM((seg_count * fan_out, seg_length, LANES), jnp.float32),
            pltpu.VMEM((2, tiles, LANES), jnp.float32),
            pltpu.VMEM((3, GX, 2 * LANES), jnp.float32),
            pltpu.VMEM((3, LANES, 2 * LANES), jnp.float32),
            pltpu.VMEM((2, passes, tiles, LANES), jnp.float32),
            pltpu.VMEM((2, tiles, tiles, LANES), jnp.float32),
            pltpu.VMEM((passes, 1, LANES), jnp.float32),
            pltpu.VMEM((tiles, 1, LANES), jnp.float32),
            pltpu.SemaphoreType.DMA((2, tiles)),
            pltpu.SemaphoreType.DMA((3, 2, passes)),
            pltpu.SemaphoreType.DMA((3, 2, tiles)),
        ],
        compiler_params=pltpu.CompilerParams(
            collective_id=0, has_side_effects=True, vmem_limit_bytes=40 * 2**20
        ),
    )(
        obs_local,
        obs_value.reshape(1, points),
        obs_weight.reshape(1, points),
        seg_tiles,
        comp_scale.reshape(1, -1),
        comp_orient.reshape(1, -1),
        comp_place.reshape(1, -1),
    )
    return coefficients.reshape(-1), field.reshape(1, 1, GX * GY)


def solution(mesh):
    return jax.shard_map(
        functools.partial(on_device, mesh.shape["tile"], mesh.shape["pass"]),
        mesh=mesh,
        in_specs=(
            P(None, None, ("tile", "pass")),
            P(("tile", "pass")),
            P(("tile", "pass")),
            P(("tile", "pass"), None),
            P("tile"),
            P("tile"),
            P("tile"),
        ),
        out_specs=(P("tile"), P("tile", "pass", None)),
        check_vma=False,
    )
```

time: 179 us -> 42.9 us (0.24)
  blocking collectives: 81.7 us -> 0 us
  Pallas kernels: 0 us -> 39.3 us
  matrix products: 34.8 us -> 0 us
  waiting for transfers between devices: 24.7 us -> 0 us
  starting transfers between devices: 22.3 us -> 0 us
  between operations: 4.83 us -> 0.7 us
  local copies, waits for them, and re-layouts: 6.67 us -> 2.69 us
  other arithmetic: 3.07 us -> 0 us
    psum x6 -> x0, blocking collectives: 72.8 us -> none  [the longest x3 55.8 us: tile_total(): return lax.psum(jnp.sum(values), 'tile')]
    pallas_call x0 -> x1, Pallas kernels: none -> 39.3 us  [on_device(): pl.pallas_call(functools.partial(kernel, tiles, passes), out_shape=(jax.S...]
    dot_general x18 -> x0, matrix products: 34.8 us -> none  [the longest x6 14.4 us: accumulate(): jnp.dot(value, slot_basis(slot_block, wavelets), precision=HIGHEST)]
    all_to_all x4 -> x0, waiting for transfers between devices: 24.7 us -> none  [the longest x2 12.5 us: on_device(): lax.all_to_all(outgoing, 'tile', split_axis=0, concat_axis=0, tiled=True)]
    all_to_all x4 -> x0, starting transfers between devices: 17.6 us -> none  [the longest x1 7.25 us: on_device(): lax.all_to_all(outgoing_points, 'tile', split_axis=1, concat_axis=1, tile...]
    all_to_all x1 -> x0, blocking collectives: 8.88 us -> none  [on_device(): lax.all_to_all(values, 'tile', split_axis=0, concat_axis=0, tiled=True)]
    ppermute x2 -> x0, starting transfers between devices: 4.77 us -> none  [the longest x1 3.25 us: with_halo(): after = lax.ppermute(initial, axis, down)]
    all_to_all x6 -> x0, local copies, waits for them, and re-layouts: 2.71 us -> none  [the longest x2 1.38 us: on_device(): lax.all_to_all(outgoing, 'tile', split_axis=0, concat_axis=0, tiled=True)]
  transfers between devices with their start and end apart: 6 -> 0, of which waited for: 4 -> 0; matrix products, arithmetic and copies ran while one was open for 2% -> 0% of each run, Pallas kernels for 0% -> 0%
where the time goes in v1:
time: 42.9 us; the launch traced here: 42.7 us
  Pallas kernels  39.3 us (92%)
  local copies, waits for them, and re-layouts  2.69 us (6%)
  between operations  0.7 us (2%)
    pallas_call x1, Pallas kernels, on_device(): pl.pallas_call(functools.partial(kernel, tiles, passes), out_shape=(jax.S...  39.3 us
    unnamed x16, local copies, waits for them, and re-layouts  2.69 us

profile of v1, /device:TPU:0, one launch (start us, length us, event | category | flops | bytes accessed | tf_op | source)
XLA Modules:
  0.0 42.7 jit_solution(8949739708286680146)
XLA Ops:
  0.6 0.0 copy-start.5
  0.6 0.7 %copy-done.5 = s32[16,2]{0,1:T(2,128)S(1)} copy-done((s32[16,2]{0,1:T(2,128)S(1)}, s32[16,2]{0,1:T(2,128)}, u32[]{:S(2)}) %copy-start.5) | copy-done | bytes 152
  1.3 0.1 copy.10.seg_ref
  1.4 0.0 copy-start
  1.4 0.0 copy-start.1
  1.4 0.0 copy-start.2
  1.4 0.0 copy-start.3
  1.4 0.0 copy-start.4
  1.4 0.8 %copy.9.obs_ref = f32[2,3,1024]{2,1,0:T(4,128)S(1)} copy(f32[2,3,1024]{2,0,1:T(2,128)} %param.7) | data formatting | bytes 49152 | tf_op args[0]
  2.2 0.0 copy-done
  2.2 0.0 copy-done.1
  2.2 0.0 copy-done.2
  2.3 0.0 copy-done.3
  2.3 0.0 copy-done.4
  2.3 39.3 %shard_map.86 = (f32[1,128]{1,0:T(1,128)S(1)}, f32[8,128]{1,0:T(8,128)S(1)}) custom-call(f32[2,3,1024]{2,1,0:T(4,128)S(1)} %copy.9.obs_ref, f32[1,1024]{1,0:T(1,128)S(1)} %bitcast.7, f32[1,1024]{1,0:T(1,128)S(1)} %bitcast.8, s32[16,2]{1,0:T(8,128)S(1)} %copy.10.seg_ref, s32[1,128]{1,0:T(1,128)S(1)} %bitcast.10, s32[1,128]{1,0:T(1,128)S(1)} %bitcast.11, ...), custom_call_target="tpu_custom_call" | custom-call | tf_op jit(solution)/shard_map/pallas_call | solution.py:287
  41.6 0.5 %copy.13 = f32[128]{0:T(128)} copy(f32[128]{0:T(128)S(1)} %bitcast.13) | data formatting | bytes 1024
  42.1 0.6 %copy.14 = f32[1,1,1024]{2,1,0:T(1,128)} copy(f32[1,1,1024]{2,1,0:T(1,128)S(1)} %bitcast.9) | data formatting | bytes 8192
Async XLA Ops:
  0.6 0.7 %copy-start.5 = (s32[16,2]{0,1:T(2,128)S(1)}, s32[16,2]{0,1:T(2,128)}, u32[]{:S(2)}) copy-start(s32[16,2]{0,1:T(2,128)} %param.10) | copy-start | bytes 388
  1.4 0.8 %copy-start = (f32[1024]{0:T(1024)S(1)}, f32[1024]{0:T(1024)}, u32[]{:S(2)}) copy-start(f32[1024]{0:T(1024)} %param.8) | copy-start | bytes 12292
  1.4 0.8 %copy-start.1 = (f32[1024]{0:T(1024)S(1)}, f32[1024]{0:T(1024)}, u32[]{:S(2)}) copy-start(f32[1024]{0:T(1024)} %param.9) | copy-start | bytes 12292
  1.4 0.9 %copy-start.2 = (s32[128]{0:T(128)S(1)}, s32[128]{0:T(128)}, u32[]{:S(2)}) copy-start(s32[128]{0:T(128)} %param.11) | copy-start | bytes 1540
  1.4 0.9 %copy-start.3 = (s32[128]{0:T(128)S(1)}, s32[128]{0:T(128)}, u32[]{:S(2)}) copy-start(s32[128]{0:T(128)} %param.12) | copy-start | bytes 1540
  1.4 0.9 %copy-start.4 = (s32[128]{0:T(128)S(1)}, s32[128]{0:T(128)}, u32[]{:S(2)}) copy-start(s32[128]{0:T(128)} %param.13) | copy-start | bytes 1540

commit v2 on v1

--- a/solution.py
+++ b/solution.py
@@ -15,7 +15,6 @@
 TIME_RATE = 8.0
 LOG2E = math.log2(math.e)
 TIME_SCALE = math.sqrt(TIME_RATE * LOG2E)
-ROUNDER = 12582912.0
 HIGHEST = lax.Precision.HIGHEST
 MESH = pl.DeviceIdType.MESH
 
@@ -57,15 +56,26 @@
 
 
 def kernel(
-    tiles, passes, obs_ref, value_ref, weight_ref, seg_ref, scale_ref, orient_ref, place_ref,
+    tiles, passes, obs_in, value_in, weight_in, seg_in, scale_in, orient_in, place_in,
     coef_ref, field_ref,
-    table, stack, columns, basis, vectors, grid_x, grid_y,
-    near, far, last_near, last_far, table_sems, near_sems, far_sems,
+    obs_ref, value_ref, weight_ref, seg_ref, scale_ref, orient_ref, place_ref, input_sems,
+    table, stack, wide, basis, vectors, grid_x, grid_y,
+    near, far, last, table_sems, near_sems, far_sems, last_sems,
 ):
     my_tile, my_pass = lax.axis_index("tile"), lax.axis_index("pass")
-    seg_count, fan_out = seg_ref.shape
+    fan_out, seg_count = seg_ref.shape
     points = value_ref.shape[1]
     seg_length = points // seg_count
+
+    inputs = [
+        pltpu.make_async_copy(source, target, input_sems.at[place])
+        for place, (source, target) in enumerate((
+            (scale_in, scale_ref), (orient_in, orient_ref), (place_in, place_ref),
+            (obs_in, obs_ref), (value_in, value_ref), (weight_in, weight_ref), (seg_in, seg_ref),
+        ))
+    ]
+    for copy in inputs:
+        copy.start()
 
     barrier = pltpu.get_barrier_semaphore()
     peers(passes, lambda d: pl.semaphore_signal(
@@ -83,6 +93,8 @@
             device_id_type=MESH,
         )
 
+    for copy in inputs[:3]:
+        copy.wait()
     level = scale_ref[...].astype(jnp.float32)
     width = 0.4 * jnp.exp(level * math.log(0.7))
     wave = 2.2 / (2.0 * math.pi) / width
@@ -100,18 +112,31 @@
     pl.semaphore_wait(barrier, passes + tiles - 2)
     peers(tiles, lambda d: to_peer(table, "tile", my_tile, tiles, table_sems, d).start())
 
-    weights = weight_ref[...]
+    for copy in inputs[3:]:
+        copy.wait()
+    roots = jnp.sqrt(weight_ref[...])
     for route in range(fan_out):
-        stack[3 * route : 3 * route + 2, :] = obs_ref[route, 0:2, :]
-        stack[3 * route + 2 : 3 * route + 3, :] = obs_ref[route, 2:3, :] * TIME_SCALE
-    stack[3 * fan_out : 3 * fan_out + 1, :] = weights
-    stack[3 * fan_out + 1 : 3 * fan_out + 2, :] = weights * value_ref[...]
-    for start in range(0, points, LANES):
-        columns[start : start + LANES, :] = stack[:, start : start + LANES].T
+        for axis in range(3):
+            line = obs_ref[axis, route : route + 1, :]
+            row = 3 * route + axis
+            stack[row : row + 1, :] = line * TIME_SCALE if axis == 2 else line
+    root_row, value_row = 3 * fan_out, 3 * fan_out + 1
+    stack[root_row : root_row + 1, :] = roots
+    stack[value_row : value_row + 1, :] = roots * value_ref[...]
+
+    def widen(block, carry):
+        start = pl.multiple_of(block * LANES, LANES)
+        columns = stack[:, pl.ds(start, LANES)].T
+        for which in range(value_row + 1):
+            wide[which, pl.ds(start, LANES), :] = jnp.broadcast_to(
+                columns[:, which : which + 1], (LANES, LANES)
+            )
+        return carry
+
+    lax.fori_loop(0, points // LANES, widen, 0)
 
     def column(seg, which):
-        rows = pl.ds(pl.multiple_of(seg * seg_length, seg_length), seg_length)
-        return jnp.broadcast_to(columns[rows, which : which + 1], (seg_length, LANES))
+        return wide[which, pl.ds(pl.multiple_of(seg * seg_length, seg_length), seg_length), :]
 
     peers(tiles, lambda d: to_peer(table, "tile", my_tile, tiles, table_sems, d).wait_recv())
 
@@ -122,9 +147,9 @@
         return running + jnp.where(tile_row == tile, part, 0.0)
 
     def build(seg, running):
-        weighted = column(seg, 3 * fan_out + 1)
+        root, weighted = column(seg, root_row), column(seg, value_row)
         for route in range(fan_out):
-            tile = seg_ref[seg, route]
+            tile = seg_ref[route, seg]
             param = lambda row: table[tile, row : row + 1, :]
             delta_x = column(seg, 3 * route) - param(0)
             delta_y = column(seg, 3 * route + 1) - param(1)
@@ -132,7 +157,7 @@
             envelope = jnp.exp2(
                 -(delta_x * delta_x + delta_y * delta_y) * param(3) - delta_t * delta_t
             )
-            phi = envelope * cos_turns(delta_x * param(4) + delta_y * param(5))
+            phi = envelope * root * cos_turns(delta_x * param(4) + delta_y * param(5))
             basis[seg * fan_out + route] = phi
             running = gather_into(running, tile, phi * weighted)
         return running
@@ -140,21 +165,21 @@
     def forward(which, seg):
         total = jnp.zeros((seg_length, LANES), jnp.float32)
         for route in range(fan_out):
-            tile = seg_ref[seg, route]
+            tile = seg_ref[route, seg]
             total = total + basis[seg * fan_out + route] * vectors[which, pl.ds(tile, 1), :]
         return jnp.sum(total, axis=1, keepdims=True)
 
     def normal(seg, running):
-        weighted = forward(0, seg) * column(seg, 3 * fan_out)
+        weighted = forward(0, seg)
         for route in range(fan_out):
             running = gather_into(
-                running, seg_ref[seg, route], basis[seg * fan_out + route] * weighted
+                running, seg_ref[route, seg], basis[seg * fan_out + route] * weighted
             )
         return running
 
     def energy(seg, running):
         values = forward(1, seg)
-        return running + values * values * column(seg, 3 * fan_out)
+        return running + values * values
 
     def sum_slots(buffer, count):
         if count <= 8:
@@ -212,7 +237,7 @@
 
     zeros = jnp.zeros((tiles, LANES), jnp.float32)
     rhs = all_sum(
-        lax.fori_loop(0, seg_count, build, zeros),
+        lax.fori_loop(0, seg_count, build, zeros, unroll=2),
         near.at[0], far.at[0], near_sems.at[0], far_sems.at[0],
         (grid_factors_x, grid_factors_y),
     )
@@ -220,7 +245,7 @@
     prior = table[:, 6, :]
     vectors[0] = rhs
     image = all_sum(
-        lax.fori_loop(0, seg_count, normal, zeros),
+        lax.fori_loop(0, seg_count, normal, zeros, unroll=8),
         near.at[1], far.at[1], near_sems.at[1], far_sems.at[1],
     ) + prior * rhs
     step_first = norm_first / total_of(rhs * image)
@@ -257,26 +282,39 @@
             fields.append(field)
 
     energies = lax.fori_loop(
-        0, seg_count, energy, jnp.zeros((seg_length, LANES), jnp.float32)
-    )
-    folded = jnp.sum(energies, axis=0, keepdims=True)
-    product = all_sum(
-        folded, last_near, last_far, near_sems.at[2], far_sems.at[2],
-        (grid_fields, lambda: None),
-    )[:, 0:1] + total_of(direction * direction * prior)
+        0, seg_count, energy, jnp.zeros((seg_length, 1), jnp.float32), unroll=8
+    )
+    me, everyone = my_tile * passes + my_pass, tiles * passes
+
+    def to_anyone(distance):
+        other = lax.rem(me + distance, everyone)
+        return pltpu.make_async_remote_copy(
+            src_ref=last.at[me],
+            dst_ref=last.at[me],
+            send_sem=last_sems.at[0, distance],
+            recv_sem=last_sems.at[1, distance],
+            device_id={"tile": other // passes, "pass": lax.rem(other, passes)},
+            device_id_type=MESH,
+        )
+
+    last[me] = jnp.broadcast_to(jnp.sum(energies, axis=0, keepdims=True), (1, LANES))
+    peers(everyone, lambda d: to_anyone(d).start())
+    grid_fields()
+    prior_product = total_of(direction * direction * prior)
+    peers(everyone, lambda d: to_anyone(d).wait_recv())
+    product = jnp.sum(last[:, 0, :], axis=0, keepdims=True)[:, 0:1] + prior_product
     step_second = norm_next / product
     mine = pl.ds(my_tile, 1)
     coef_ref[...] = step_first * vectors[0, mine, :] + step_second * vectors[1, mine, :]
     field_ref[...] = step_first * fields[0] + step_second * fields[1]
 
     peers(tiles, lambda d: to_peer(table, "tile", my_tile, tiles, table_sems, d).wait_send())
-    for stage in range(3):
-        near_slots = near.at[stage] if stage < 2 else last_near
-        far_slots = far.at[stage] if stage < 2 else last_far
+    for stage in range(2):
         peers(passes, lambda d: to_peer(
-            near_slots, "pass", my_pass, passes, near_sems.at[stage], d).wait_send())
+            near.at[stage], "pass", my_pass, passes, near_sems.at[stage], d).wait_send())
         peers(tiles, lambda d: to_peer(
-            far_slots, "tile", my_tile, tiles, far_sems.at[stage], d).wait_send())
+            far.at[stage], "tile", my_tile, tiles, far_sems.at[stage], d).wait_send())
+    peers(everyone, lambda d: to_anyone(d).wait_send())
 
 
 def on_device(tiles, passes, obs_local, obs_value, obs_weight, seg_tiles, comp_scale, comp_orient, comp_place):
@@ -290,32 +328,40 @@
             jax.ShapeDtypeStruct((1, LANES), jnp.float32),
             jax.ShapeDtypeStruct((8, LANES), jnp.float32),
         ),
-        in_specs=[vmem, vmem, vmem, pl.BlockSpec(memory_space=pltpu.SMEM), vmem, vmem, vmem],
+        in_specs=[pl.BlockSpec(memory_space=pl.ANY)] * 7,
         out_specs=(vmem, vmem),
         scratch_shapes=[
+            pltpu.VMEM((3, fan_out, points), jnp.float32),
+            pltpu.VMEM((1, points), jnp.float32),
+            pltpu.VMEM((1, points), jnp.float32),
+            pltpu.SMEM((fan_out, seg_count), jnp.int32),
+            pltpu.VMEM((1, LANES), jnp.int32),
+            pltpu.VMEM((1, LANES), jnp.int32),
+            pltpu.VMEM((1, LANES), jnp.int32),
+            pltpu.SemaphoreType.DMA((7,)),
             pltpu.VMEM((tiles, 8, LANES), jnp.float32),
-            pltpu.VMEM((8, points), jnp.float32),
-            pltpu.VMEM((points, 8), jnp.float32),
+            pltpu.VMEM((3 * fan_out + 2, points), jnp.float32),
+            pltpu.VMEM((3 * fan_out + 2, points, LANES), jnp.float32),
             pltpu.VMEM((seg_count * fan_out, seg_length, LANES), jnp.float32),
             pltpu.VMEM((2, tiles, LANES), jnp.float32),
             pltpu.VMEM((3, GX, 2 * LANES), jnp.float32),
             pltpu.VMEM((3, LANES, 2 * LANES), jnp.float32),
             pltpu.VMEM((2, passes, tiles, LANES), jnp.float32),
             pltpu.VMEM((2, tiles, tiles, LANES), jnp.float32),
-            pltpu.VMEM((passes, 1, LANES), jnp.float32),
-            pltpu.VMEM((tiles, 1, LANES), jnp.float32),
+            pltpu.VMEM((tiles * passes, 1, LANES), jnp.float32),
             pltpu.SemaphoreType.DMA((2, tiles)),
-            pltpu.SemaphoreType.DMA((3, 2, passes)),
-            pltpu.SemaphoreType.DMA((3, 2, tiles)),
+            pltpu.SemaphoreType.DMA((2, 2, passes)),
+            pltpu.SemaphoreType.DMA((2, 2, tiles)),
+            pltpu.SemaphoreType.DMA((2, tiles * passes)),
         ],
         compiler_params=pltpu.CompilerParams(
-            collective_id=0, has_side_effects=True, vmem_limit_bytes=40 * 2**20
+            collective_id=0, has_side_effects=True, vmem_limit_bytes=60 * 2**20
         ),
     )(
-        obs_local,
+        obs_local.transpose(1, 0, 2),
         obs_value.reshape(1, points),
         obs_weight.reshape(1, points),
-        seg_tiles,
+        seg_tiles.T,
         comp_scale.reshape(1, -1),
         comp_orient.reshape(1, -1),
         comp_place.reshape(1, -1),

time: 42.9 us -> 35.5 us (0.83)
  Pallas kernels: 39.3 us -> 32.9 us
  local copies, waits for them, and re-layouts: 2.69 us -> 1.74 us
    pallas_call x1, Pallas kernels: 39.3 us -> 32.9 us  [on_device(): pl.pallas_call(functools.partial(kernel, tiles, passes), out_shape=(jax.S...]
    unnamed x16 -> x6, local copies, waits for them, and re-layouts: 2.69 us -> 1.74 us
where the time goes in v2:
time: 35.5 us; the launch traced here: 35.3 us
  Pallas kernels  32.9 us (93%)
  local copies, waits for them, and re-layouts  1.74 us (5%)
  between operations  0.66 us (2%)
    pallas_call x1, Pallas kernels, on_device(): pl.pallas_call(functools.partial(kernel, tiles, passes), out_shape=(jax.S...  32.9 us
    unnamed x6, local copies, waits for them, and re-layouts  1.74 us

profile of v2, /device:TPU:0, one launch (start us, length us, event | category | flops | bytes accessed | tf_op | source)
XLA Modules:
  0.0 35.3 jit_solution(11385958104296340364)
XLA Ops:
  0.6 32.9 %shard_map.86 = (f32[1,128]{1,0:T(1,128)}, f32[8,128]{1,0:T(8,128)}) custom-call(f32[3,2,1024]{2,1,0:T(2,128)} %bitcast.9, f32[1,1024]{1,0:T(1,128)} %bitcast.10, f32[1,1024]{1,0:T(1,128)} %bitcast.11, s32[2,16]{1,0:T(2,128)} %bitcast.13, s32[1,128]{1,0:T(1,128)} %bitcast.14, s32[1,128]{1,0:T(1,128)} %bitcast.15, s32[1,128]{1,0:T(1,128)} %bitcast.16), custom_call_target="tpu_custom_call" | custom-call | tf_op jit(solution)/shard_map/pallas_call | solution.py:325
  33.5 0.0 copy-start
  33.6 0.0 copy-start.1
  33.6 0.6 %copy-done.1 = f32[1,128]{1,0:T(1,128)S(1)} copy-done((f32[1,128]{1,0:T(1,128)S(1)}, f32[1,128]{1,0:T(1,128)}, u32[]{:S(2)}) %copy-start.1) | copy-done | bytes 536
  34.2 0.5 %copy.11 = f32[128]{0:T(128)} copy(f32[128]{0:T(128)S(1)} %bitcast.17) | data formatting | bytes 1024
  34.7 0.0 copy-done
  34.7 0.6 %copy.12 = f32[1,1,1024]{2,1,0:T(1,128)} copy(f32[1,1,1024]{2,1,0:T(1,128)S(1)} %bitcast.12) | data formatting | bytes 8192
Async XLA Ops:
  33.5 1.2 %copy-start = (f32[8,128]{1,0:T(8,128)S(1)}, f32[8,128]{1,0:T(8,128)}, u32[]{:S(2)}) copy-start(f32[8,128]{1,0:T(8,128)} %get-tuple-element.5) | copy-start | bytes 12292
  33.6 0.6 %copy-start.1 = (f32[1,128]{1,0:T(1,128)S(1)}, f32[1,128]{1,0:T(1,128)}, u32[]{:S(2)}) copy-start(f32[1,128]{1,0:T(1,128)} %get-tuple-element.4) | copy-start | bytes 1540

commit v3 on v2

--- a/solution.py
+++ b/solution.py
@@ -39,7 +39,7 @@
 
 
 def peers(count, body):
-    if count <= 8:
+    if count <= 32:
         for distance in range(1, count):
             body(distance)
     else:
@@ -87,14 +87,18 @@
         return pltpu.make_async_remote_copy(
             src_ref=buffer.at[me],
             dst_ref=buffer.at[me],
-            send_sem=sems.at[0, distance],
-            recv_sem=sems.at[1, distance],
+            send_sem=sems.at[0],
+            recv_sem=sems.at[1],
             device_id={axis: lax.rem(me + distance, count)},
             device_id_type=MESH,
         )
 
     for copy in inputs[:3]:
         copy.wait()
+    def wait_for_peers(buffer, count, sem):
+        slots = buffer.at[pl.ds(0, count - 1)]
+        pltpu.make_async_copy(slots, slots, sem).wait()
+
     level = scale_ref[...].astype(jnp.float32)
     width = 0.4 * jnp.exp(level * math.log(0.7))
     wave = 2.2 / (2.0 * math.pi) / width
@@ -133,12 +137,12 @@
             )
         return carry
 
-    lax.fori_loop(0, points // LANES, widen, 0)
+    lax.fori_loop(0, points // LANES, widen, 0, unroll=4)
 
     def column(seg, which):
         return wide[which, pl.ds(pl.multiple_of(seg * seg_length, seg_length), seg_length), :]
 
-    peers(tiles, lambda d: to_peer(table, "tile", my_tile, tiles, table_sems, d).wait_recv())
+    wait_for_peers(table, tiles, table_sems.at[1])
 
     tile_row = lax.broadcasted_iota(jnp.int32, (tiles, LANES), 0)
 
@@ -194,12 +198,12 @@
         peers(passes, lambda d: to_peer(near_slots, "pass", my_pass, passes, near_sem, d).start())
         if beside is not None:
             beside[0]()
-        peers(passes, lambda d: to_peer(near_slots, "pass", my_pass, passes, near_sem, d).wait_recv())
+        wait_for_peers(near_slots, passes, near_sem.at[1])
         far_slots[my_tile] = sum_slots(near_slots, passes)
         peers(tiles, lambda d: to_peer(far_slots, "tile", my_tile, tiles, far_sem, d).start())
         if beside is not None:
             beside[1]()
-        peers(tiles, lambda d: to_peer(far_slots, "tile", my_tile, tiles, far_sem, d).wait_recv())
+        wait_for_peers(far_slots, tiles, far_sem.at[1])
         return sum_slots(far_slots, tiles)
 
     def grid_params(neighbor):
@@ -237,17 +241,18 @@
 
     zeros = jnp.zeros((tiles, LANES), jnp.float32)
     rhs = all_sum(
-        lax.fori_loop(0, seg_count, build, zeros, unroll=2),
+        lax.fori_loop(0, seg_count, build, zeros, unroll=4),
         near.at[0], far.at[0], near_sems.at[0], far_sems.at[0],
         (grid_factors_x, grid_factors_y),
     )
-    norm_first = total_of(rhs * rhs)
-    prior = table[:, 6, :]
+    prior, norms = table[:, 6, :], []
     vectors[0] = rhs
     image = all_sum(
         lax.fori_loop(0, seg_count, normal, zeros, unroll=8),
         near.at[1], far.at[1], near_sems.at[1], far_sems.at[1],
+        (lambda: norms.append(total_of(rhs * rhs)), lambda: None),
     ) + prior * rhs
+    norm_first = norms[0]
     step_first = norm_first / total_of(rhs * image)
     residual = rhs - step_first * image
     norm_next = total_of(residual * residual)
@@ -291,8 +296,8 @@
         return pltpu.make_async_remote_copy(
             src_ref=last.at[me],
             dst_ref=last.at[me],
-            send_sem=last_sems.at[0, distance],
-            recv_sem=last_sems.at[1, distance],
+            send_sem=last_sems.at[0],
+            recv_sem=last_sems.at[1],
             device_id={"tile": other // passes, "pass": lax.rem(other, passes)},
             device_id_type=MESH,
         )
@@ -301,20 +306,29 @@
     peers(everyone, lambda d: to_anyone(d).start())
     grid_fields()
     prior_product = total_of(direction * direction * prior)
-    peers(everyone, lambda d: to_anyone(d).wait_recv())
+    wait_for_peers(last, everyone, last_sems.at[1])
     product = jnp.sum(last[:, 0, :], axis=0, keepdims=True)[:, 0:1] + prior_product
     step_second = norm_next / product
     mine = pl.ds(my_tile, 1)
     coef_ref[...] = step_first * vectors[0, mine, :] + step_second * vectors[1, mine, :]
     field_ref[...] = step_first * fields[0] + step_second * fields[1]
 
-    peers(tiles, lambda d: to_peer(table, "tile", my_tile, tiles, table_sems, d).wait_send())
+    wait_for_peers(table, tiles, table_sems.at[0])
     for stage in range(2):
-        peers(passes, lambda d: to_peer(
-            near.at[stage], "pass", my_pass, passes, near_sems.at[stage], d).wait_send())
-        peers(tiles, lambda d: to_peer(
-            far.at[stage], "tile", my_tile, tiles, far_sems.at[stage], d).wait_send())
-    peers(everyone, lambda d: to_anyone(d).wait_send())
+        wait_for_peers(near.at[stage], passes, near_sems.at[stage, 0])
+        wait_for_peers(far.at[stage], tiles, far_sems.at[stage, 0])
+    wait_for_peers(last, everyone, last_sems.at[0])
+
+
+def hand_over(coef_in, field_in, coef_ref, field_ref, sems):
+    copies = [
+        pltpu.make_async_copy(coef_in, coef_ref, sems.at[0]),
+        pltpu.make_async_copy(field_in, field_ref, sems.at[1]),
+    ]
+    for copy in copies:
+        copy.start()
+    for copy in copies:
+        copy.wait()
 
 
 def on_device(tiles, passes, obs_local, obs_value, obs_weight, seg_tiles, comp_scale, comp_orient, comp_place):
@@ -349,10 +363,10 @@
             pltpu.VMEM((2, passes, tiles, LANES), jnp.float32),
             pltpu.VMEM((2, tiles, tiles, LANES), jnp.float32),
             pltpu.VMEM((tiles * passes, 1, LANES), jnp.float32),
-            pltpu.SemaphoreType.DMA((2, tiles)),
-            pltpu.SemaphoreType.DMA((2, 2, passes)),
-            pltpu.SemaphoreType.DMA((2, 2, tiles)),
-            pltpu.SemaphoreType.DMA((2, tiles * passes)),
+            pltpu.SemaphoreType.DMA((2,)),
+            pltpu.SemaphoreType.DMA((2, 2)),
+            pltpu.SemaphoreType.DMA((2, 2)),
+            pltpu.SemaphoreType.DMA((2,)),
         ],
         compiler_params=pltpu.CompilerParams(
             collective_id=0, has_side_effects=True, vmem_limit_bytes=60 * 2**20
@@ -366,6 +380,18 @@
         comp_orient.reshape(1, -1),
         comp_place.reshape(1, -1),
     )
+    anywhere = pl.BlockSpec(memory_space=pl.ANY)
+    coefficients, field = pl.pallas_call(
+        hand_over,
+        out_shape=(
+            jax.ShapeDtypeStruct((1, LANES), jnp.float32),
+            jax.ShapeDtypeStruct((8, LANES), jnp.float32),
+        ),
+        in_specs=[anywhere, anywhere],
+        out_specs=(anywhere, anywhere),
+        scratch_shapes=[pltpu.SemaphoreType.DMA((2,))],
+        compiler_params=pltpu.CompilerParams(vmem_limit_bytes=60 * 2**20),
+    )(coefficients, field)
     return coefficients.reshape(-1), field.reshape(1, 1, GX * GY)
 
 

time: 35.5 us -> 33.4 us (0.941)
  local copies, waits for them, and re-layouts: 1.74 us -> 0 us
    unnamed x6 -> x0, local copies, waits for them, and re-layouts: 1.74 us -> none
    pallas_call x1, Pallas kernels: 32.9 us -> 31.3 us  [on_device(): pl.pallas_call(functools.partial(kernel, tiles, passes), out_shape=(jax.S...]
    pallas_call x0 -> x1, Pallas kernels: none -> 1.26 us  [on_device(): pl.pallas_call(hand_over, out_shape=(jax.ShapeDtypeStruct((1, LANES), jnp...]
where the time goes in v3:
time: 33.4 us; the launch traced here: 33.2 us
  Pallas kernels  32.6 us (98%)
  between operations  0.64 us (2%)
    pallas_call x1, Pallas kernels, on_device(): pl.pallas_call(functools.partial(kernel, tiles, passes), out_shape=(jax.S...  31.3 us
    pallas_call x1, Pallas kernels, on_device(): pl.pallas_call(hand_over, out_shape=(jax.ShapeDtypeStruct((1, LANES), jnp...  1.26 us

profile of v3, /device:TPU:0, one launch (start us, length us, event | category | flops | bytes accessed | tf_op | source)
XLA Modules:
  0.0 33.2 jit_solution(9156844235500510150)
XLA Ops:
  0.6 31.3 %shard_map.86 = (f32[1,128]{1,0:T(1,128)}, f32[8,128]{1,0:T(8,128)}) custom-call(f32[3,2,1024]{2,1,0:T(2,128)} %bitcast.9, f32[1,1024]{1,0:T(1,128)} %bitcast.10, f32[1,1024]{1,0:T(1,128)} %bitcast.11, s32[2,16]{1,0:T(2,128)} %bitcast.12, s32[1,128]{1,0:T(1,128)} %bitcast.13, s32[1,128]{1,0:T(1,128)} %bitcast.14, s32[1,128]{1,0:T(1,128)} %bitcast.15), custom_call_target="tpu_custom_call" | custom-call | tf_op jit(solution)/shard_map/pallas_call | solution.py:339
  31.9 1.3 %shard_map.87 = (f32[1,128]{1,0:T(1,128)}, f32[8,128]{1,0:T(8,128)}) custom-call(f32[1,128]{1,0:T(1,128)} %get-tuple-element.6.coef_in, f32[8,128]{1,0:T(8,128)} %get-tuple-element.7.field_in), custom_call_target="tpu_custom_call" | custom-call | tf_op jit(solution)/shard_map/pallas_call | solution.py:384

commit v4 on v3

--- a/solution.py
+++ b/solution.py
@@ -13,8 +13,7 @@
 GY = 32
 LANES = 128
 TIME_RATE = 8.0
-LOG2E = math.log2(math.e)
-TIME_SCALE = math.sqrt(TIME_RATE * LOG2E)
+TIME_SCALE = math.sqrt(TIME_RATE)
 HIGHEST = lax.Precision.HIGHEST
 MESH = pl.DeviceIdType.MESH
 
@@ -56,9 +55,8 @@
 
 
 def kernel(
-    tiles, passes, obs_in, value_in, weight_in, seg_in, scale_in, orient_in, place_in,
+    tiles, passes, obs_ref, value_ref, weight_ref, seg_ref, scale_ref, orient_ref, place_ref,
     coef_ref, field_ref,
-    obs_ref, value_ref, weight_ref, seg_ref, scale_ref, orient_ref, place_ref, input_sems,
     table, stack, wide, basis, vectors, grid_x, grid_y,
     near, far, last, table_sems, near_sems, far_sems, last_sems,
 ):
@@ -66,16 +64,6 @@
     fan_out, seg_count = seg_ref.shape
     points = value_ref.shape[1]
     seg_length = points // seg_count
-
-    inputs = [
-        pltpu.make_async_copy(source, target, input_sems.at[place])
-        for place, (source, target) in enumerate((
-            (scale_in, scale_ref), (orient_in, orient_ref), (place_in, place_ref),
-            (obs_in, obs_ref), (value_in, value_ref), (weight_in, weight_ref), (seg_in, seg_ref),
-        ))
-    ]
-    for copy in inputs:
-        copy.start()
 
     barrier = pltpu.get_barrier_semaphore()
     peers(passes, lambda d: pl.semaphore_signal(
@@ -93,8 +81,6 @@
             device_id_type=MESH,
         )
 
-    for copy in inputs[:3]:
-        copy.wait()
     def wait_for_peers(buffer, count, sem):
         slots = buffer.at[pl.ds(0, count - 1)]
         pltpu.make_async_copy(slots, slots, sem).wait()
@@ -107,7 +93,7 @@
     table[my_tile, 0:1, :] = ((place & 7).astype(jnp.float32) + 0.5) / 8.0
     table[my_tile, 1:2, :] = (((place >> 3) & 7).astype(jnp.float32) + 0.5) / 8.0
     table[my_tile, 2:3, :] = ((place >> 6).astype(jnp.float32) + 0.5) * (TIME_SCALE / 8.0)
-    table[my_tile, 3:4, :] = 0.5 * LOG2E / (width * width)
+    table[my_tile, 3:4, :] = 0.5 / (width * width)
     table[my_tile, 4:5, :] = wave * cos_turns(turns)
     table[my_tile, 5:6, :] = wave * cos_turns(turns - 0.25)
     table[my_tile, 6:7, :] = 2.0 * jnp.exp(level * math.log(1.5))
@@ -116,8 +102,6 @@
     pl.semaphore_wait(barrier, passes + tiles - 2)
     peers(tiles, lambda d: to_peer(table, "tile", my_tile, tiles, table_sems, d).start())
 
-    for copy in inputs[3:]:
-        copy.wait()
     roots = jnp.sqrt(weight_ref[...])
     for route in range(fan_out):
         for axis in range(3):
@@ -158,7 +142,7 @@
             delta_x = column(seg, 3 * route) - param(0)
             delta_y = column(seg, 3 * route + 1) - param(1)
             delta_t = column(seg, 3 * route + 2) - param(2)
-            envelope = jnp.exp2(
+            envelope = jnp.exp(
                 -(delta_x * delta_x + delta_y * delta_y) * param(3) - delta_t * delta_t
             )
             phi = envelope * root * cos_turns(delta_x * param(4) + delta_y * param(5))
@@ -211,7 +195,7 @@
         return tile, lambda row: table[tile, row : row + 1, :]
 
     def axis_factors(delta, inverse, wave_row):
-        envelope = jnp.exp2(-(delta * delta) * inverse)
+        envelope = jnp.exp(-(delta * delta) * inverse)
         phase = delta * wave_row
         return envelope * cos_turns(phase), envelope * cos_turns(phase - 0.25)
 
@@ -235,9 +219,28 @@
                 place_x - (param(0) + float(neighbor - 1)), param(3), param(4)
             )
             delta_t = day - param(2)
-            in_time = jnp.exp2(-(delta_t * delta_t))
+            in_time = jnp.exp(-(delta_t * delta_t))
             grid_x[neighbor, :, :LANES] = even * in_time
             grid_x[neighbor, :, LANES:] = -odd * in_time
+
+    def grid_field(which):
+        total = None
+        for neighbor in range(3):
+            tile, _ = grid_params(neighbor)
+            row = vectors[which, pl.ds(tile, 1), :]
+            term = lax.dot_general(
+                grid_x[neighbor] * jnp.concatenate([row, row], axis=1),
+                grid_y[neighbor],
+                (((1,), (1,)), ((), ())),
+                precision=HIGHEST,
+                preferred_element_type=jnp.float32,
+            )
+            total = term if total is None else total + term
+        group = lax.broadcasted_iota(jnp.int32, (8, LANES), 1) // GY
+        field = jnp.zeros((8, LANES), jnp.float32)
+        for part in range(GX // 8):
+            field = field + jnp.where(group == part, total[8 * part : 8 * part + 8, :], 0.0)
+        return field
 
     zeros = jnp.zeros((tiles, LANES), jnp.float32)
     rhs = all_sum(
@@ -245,12 +248,12 @@
         near.at[0], far.at[0], near_sems.at[0], far_sems.at[0],
         (grid_factors_x, grid_factors_y),
     )
-    prior, norms = table[:, 6, :], []
+    prior, norms, fields = table[:, 6, :], [], []
     vectors[0] = rhs
     image = all_sum(
         lax.fori_loop(0, seg_count, normal, zeros, unroll=8),
         near.at[1], far.at[1], near_sems.at[1], far_sems.at[1],
-        (lambda: norms.append(total_of(rhs * rhs)), lambda: None),
+        (lambda: norms.append(total_of(rhs * rhs)), lambda: fields.append(grid_field(0))),
     ) + prior * rhs
     norm_first = norms[0]
     step_first = norm_first / total_of(rhs * image)
@@ -258,33 +261,6 @@
     norm_next = total_of(residual * residual)
     direction = residual + norm_next / norm_first * rhs
     vectors[1] = direction
-
-    fields = []
-
-    def grid_fields():
-        total = None
-        for neighbor in range(3):
-            tile, _ = grid_params(neighbor)
-            parts = []
-            for which in range(2):
-                row = vectors[which, pl.ds(tile, 1), :]
-                parts.append(grid_x[neighbor] * jnp.concatenate([row, row], axis=1))
-            term = lax.dot_general(
-                jnp.concatenate(parts, axis=0),
-                grid_y[neighbor],
-                (((1,), (1,)), ((), ())),
-                precision=HIGHEST,
-                preferred_element_type=jnp.float32,
-            )
-            total = term if total is None else total + term
-        group = lax.broadcasted_iota(jnp.int32, (8, LANES), 1) // GY
-        for begin in (0, GX):
-            field = jnp.zeros((8, LANES), jnp.float32)
-            for part in range(GX // 8):
-                field = field + jnp.where(
-                    group == part, total[begin + 8 * part : begin + 8 * part + 8, :], 0.0
-                )
-            fields.append(field)
 
     energies = lax.fori_loop(
         0, seg_count, energy, jnp.zeros((seg_length, 1), jnp.float32), unroll=8
@@ -304,7 +280,7 @@
 
     last[me] = jnp.broadcast_to(jnp.sum(energies, axis=0, keepdims=True), (1, LANES))
     peers(everyone, lambda d: to_anyone(d).start())
-    grid_fields()
+    fields.append(grid_field(1))
     prior_product = total_of(direction * direction * prior)
     wait_for_peers(last, everyone, last_sems.at[1])
     product = jnp.sum(last[:, 0, :], axis=0, keepdims=True)[:, 0:1] + prior_product
@@ -336,23 +312,16 @@
     points = obs_value.shape[0]
     seg_length = points // seg_count
     vmem = pl.BlockSpec(memory_space=pltpu.VMEM)
+    hbm = pl.BlockSpec(memory_space=pltpu.HBM)
     coefficients, field = pl.pallas_call(
         functools.partial(kernel, tiles, passes),
         out_shape=(
             jax.ShapeDtypeStruct((1, LANES), jnp.float32),
             jax.ShapeDtypeStruct((8, LANES), jnp.float32),
         ),
-        in_specs=[pl.BlockSpec(memory_space=pl.ANY)] * 7,
+        in_specs=[vmem, vmem, vmem, pl.BlockSpec(memory_space=pltpu.SMEM), vmem, vmem, vmem],
         out_specs=(vmem, vmem),
         scratch_shapes=[
-            pltpu.VMEM((3, fan_out, points), jnp.float32),
-            pltpu.VMEM((1, points), jnp.float32),
-            pltpu.VMEM((1, points), jnp.float32),
-            pltpu.SMEM((fan_out, seg_count), jnp.int32),
-            pltpu.VMEM((1, LANES), jnp.int32),
-            pltpu.VMEM((1, LANES), jnp.int32),
-            pltpu.VMEM((1, LANES), jnp.int32),
-            pltpu.SemaphoreType.DMA((7,)),
             pltpu.VMEM((tiles, 8, LANES), jnp.float32),
             pltpu.VMEM((3 * fan_out + 2, points), jnp.float32),
             pltpu.VMEM((3 * fan_out + 2, points, LANES), jnp.float32),
@@ -369,7 +338,7 @@
             pltpu.SemaphoreType.DMA((2,)),
         ],
         compiler_params=pltpu.CompilerParams(
-            collective_id=0, has_side_effects=True, vmem_limit_bytes=60 * 2**20
+            collective_id=0, has_side_effects=True, vmem_limit_bytes=40 * 2**20
         ),
     )(
         obs_local.transpose(1, 0, 2),
@@ -380,17 +349,15 @@
         comp_orient.reshape(1, -1),
         comp_place.reshape(1, -1),
     )
-    anywhere = pl.BlockSpec(memory_space=pl.ANY)
     coefficients, field = pl.pallas_call(
         hand_over,
         out_shape=(
             jax.ShapeDtypeStruct((1, LANES), jnp.float32),
             jax.ShapeDtypeStruct((8, LANES), jnp.float32),
         ),
-        in_specs=[anywhere, anywhere],
-        out_specs=(anywhere, anywhere),
+        in_specs=[vmem, vmem],
+        out_specs=(hbm, hbm),
         scratch_shapes=[pltpu.SemaphoreType.DMA((2,))],
-        compiler_params=pltpu.CompilerParams(vmem_limit_bytes=60 * 2**20),
     )(coefficients, field)
     return coefficients.reshape(-1), field.reshape(1, 1, GX * GY)
 

time: 33.4 us -> 36 us (1.078)
  local copies, waits for them, and re-layouts: 0 us -> 2.6 us
    unnamed x0 -> x18, local copies, waits for them, and re-layouts: none -> 2.6 us
where the time goes in v4:
time: 36 us; the launch traced here: 35.8 us
  Pallas kernels  32.5 us (90%)
  local copies, waits for them, and re-layouts  2.6 us (7%)
  between operations  0.7 us (2%)
    pallas_call x1, Pallas kernels, on_device(): pl.pallas_call(functools.partial(kernel, tiles, passes), out_shape=(jax.S...  31.2 us
    unnamed x18, local copies, waits for them, and re-layouts  2.6 us
    pallas_call x1, Pallas kernels, on_device(): pl.pallas_call(hand_over, out_shape=(jax.ShapeDtypeStruct((1, LANES), jnp...  1.3 us

profile of v4, /device:TPU:0, one launch (start us, length us, event | category | flops | bytes accessed | tf_op | source)
XLA Modules:
  0.0 35.8 jit_solution(6378582117360835786)
XLA Ops:
  0.6 0.0 copy-start.5
  0.6 0.0 copy-start.6
  0.7 0.0 copy-start.7
  0.7 0.0 copy-start.2
  0.7 0.0 copy-start.1
  0.7 0.0 copy-start.4
  0.7 0.6 %copy-done.5 = s32[128]{0:T(128)S(1)} copy-done((s32[128]{0:T(128)S(1)}, s32[128]{0:T(128)}, u32[]{:S(2)}) %copy-start.5) | copy-done | bytes 536
  1.3 0.0 copy-done.6
  1.3 0.0 copy-done.7
  1.3 0.0 copy-done.2
  1.4 0.0 copy-done.1
  1.4 0.0 copy-done.4
  1.4 0.0 copy-start
  1.4 0.7 %copy-done = f32[2,3,1024]{2,0,1:T(2,128)S(1)} copy-done((f32[2,3,1024]{2,0,1:T(2,128)S(1)}, f32[2,3,1024]{2,0,1:T(2,128)}, u32[]{:S(2)}) %copy-start) | copy-done | bytes 24600
  2.1 31.2 %shard_map.86 = (f32[1,128]{1,0:T(1,128)S(1)}, f32[8,128]{1,0:T(8,128)S(1)}) custom-call(f32[3,2,1024]{2,1,0:T(2,128)S(1)} %bitcast.9, f32[1,1024]{1,0:T(1,128)S(1)} %bitcast.10, f32[1,1024]{1,0:T(1,128)S(1)} %bitcast.11, s32[2,16]{1,0:T(2,128)S(1)} %bitcast.12, s32[1,128]{1,0:T(1,128)S(1)} %bitcast.13, s32[1,128]{1,0:T(1,128)S(1)} %bitcast.14, ...), custom_call_target="tpu_custom_call" | custom-call | tf_op jit(solution)/shard_map/pallas_call | solution.py:316
  33.3 0.0 copy-start.3
  33.3 0.6 %copy-done.3 = f32[8,128]{1,0:T(8,128)} copy-done((f32[8,128]{1,0:T(8,128)}, f32[8,128]{1,0:T(8,128)S(1)}, u32[]{:S(2)}) %copy-start.3) | copy-done | bytes 4120
  33.9 0.0 copy-start.8
  33.9 0.6 %copy-done.8 = f32[1,128]{1,0:T(1,128)} copy-done((f32[1,128]{1,0:T(1,128)}, f32[1,128]{1,0:T(1,128)S(1)}, u32[]{:S(2)}) %copy-start.8) | copy-done | bytes 536
  34.5 1.3 %shard_map.87 = (f32[1,128]{1,0:T(1,128)}, f32[8,128]{1,0:T(8,128)}) custom-call(f32[1,128]{1,0:T(1,128)} %copy-done.8, f32[8,128]{1,0:T(8,128)} %copy-done.3), custom_call_target="tpu_custom_call" | custom-call | tf_op jit(solution)/shard_map/pallas_call | solution.py:352
Async XLA Ops:
  0.6 0.7 %copy-start.5 = (s32[128]{0:T(128)S(1)}, s32[128]{0:T(128)}, u32[]{:S(2)}) copy-start(s32[128]{0:T(128)} %param.11) | copy-start | bytes 1540
  0.6 0.7 %copy-start.6 = (s32[128]{0:T(128)S(1)}, s32[128]{0:T(128)}, u32[]{:S(2)}) copy-start(s32[128]{0:T(128)} %param.12) | copy-start | bytes 1540
  0.7 0.7 %copy-start.7 = (s32[128]{0:T(128)S(1)}, s32[128]{0:T(128)}, u32[]{:S(2)}) copy-start(s32[128]{0:T(128)} %param.13) | copy-start | bytes 1540
  0.7 0.7 %copy-start.2 = (f32[1024]{0:T(1024)S(1)}, f32[1024]{0:T(1024)}, u32[]{:S(2)}) copy-start(f32[1024]{0:T(1024)} %param.9) | copy-start | bytes 12292
  0.7 0.7 %copy-start.1 = (f32[1024]{0:T(1024)S(1)}, f32[1024]{0:T(1024)}, u32[]{:S(2)}) copy-start(f32[1024]{0:T(1024)} %param.8) | copy-start | bytes 12292
  0.7 0.7 %copy-start.4 = (s32[16,2]{0,1:T(2,128)S(1)}, s32[16,2]{0,1:T(2,128)}, u32[]{:S(2)}) copy-start(s32[16,2]{0,1:T(2,128)} %param.10) | copy-start | bytes 388
  1.4 0.7 %copy-start = (f32[2,3,1024]{2,0,1:T(2,128)S(1)}, f32[2,3,1024]{2,0,1:T(2,128)}, u32[]{:S(2)}) copy-start(f32[2,3,1024]{2,0,1:T(2,128)} %param.7) | copy-start | bytes 73732
  33.3 0.6 %copy-start.3 = (f32[8,128]{1,0:T(8,128)}, f32[8,128]{1,0:T(8,128)S(1)}, u32[]{:S(2)}) copy-start(f32[8,128]{1,0:T(8,128)S(1)} %get-tuple-element.7.field_in) | copy-start | bytes 12292
  33.9 0.6 %copy-start.8 = (f32[1,128]{1,0:T(1,128)}, f32[1,128]{1,0:T(1,128)S(1)}, u32[]{:S(2)}) copy-start(f32[1,128]{1,0:T(1,128)S(1)} %get-tuple-element.6.coef_in) | copy-start | bytes 1540

commit v5 on v3

--- a/solution.py
+++ b/solution.py
@@ -13,9 +13,7 @@
 GY = 32
 LANES = 128
 TIME_RATE = 8.0
-LOG2E = math.log2(math.e)
-TIME_SCALE = math.sqrt(TIME_RATE * LOG2E)
-HIGHEST = lax.Precision.HIGHEST
+TIME_SCALE = math.sqrt(TIME_RATE)
 MESH = pl.DeviceIdType.MESH
 
 
@@ -49,6 +47,11 @@
             return carry
 
         lax.fori_loop(1, count, step, 0)
+
+
+def split(value):
+    high = value.astype(jnp.bfloat16)
+    return high, (value - high.astype(jnp.float32)).astype(jnp.bfloat16)
 
 
 def total_of(value):
@@ -67,6 +70,12 @@
     points = value_ref.shape[1]
     seg_length = points // seg_count
 
+    barrier = pltpu.get_barrier_semaphore()
+    peers(passes, lambda d: pl.semaphore_signal(
+        barrier, inc=1, device_id={"pass": lax.rem(my_pass + d, passes)}, device_id_type=MESH))
+    peers(tiles, lambda d: pl.semaphore_signal(
+        barrier, inc=1, device_id={"tile": lax.rem(my_tile + d, tiles)}, device_id_type=MESH))
+
     inputs = [
         pltpu.make_async_copy(source, target, input_sems.at[place])
         for place, (source, target) in enumerate((
@@ -77,12 +86,6 @@
     for copy in inputs:
         copy.start()
 
-    barrier = pltpu.get_barrier_semaphore()
-    peers(passes, lambda d: pl.semaphore_signal(
-        barrier, inc=1, device_id={"pass": lax.rem(my_pass + d, passes)}, device_id_type=MESH))
-    peers(tiles, lambda d: pl.semaphore_signal(
-        barrier, inc=1, device_id={"tile": lax.rem(my_tile + d, tiles)}, device_id_type=MESH))
-
     def to_peer(buffer, axis, me, count, sems, distance):
         return pltpu.make_async_remote_copy(
             src_ref=buffer.at[me],
@@ -107,7 +110,7 @@
     table[my_tile, 0:1, :] = ((place & 7).astype(jnp.float32) + 0.5) / 8.0
     table[my_tile, 1:2, :] = (((place >> 3) & 7).astype(jnp.float32) + 0.5) / 8.0
     table[my_tile, 2:3, :] = ((place >> 6).astype(jnp.float32) + 0.5) * (TIME_SCALE / 8.0)
-    table[my_tile, 3:4, :] = 0.5 * LOG2E / (width * width)
+    table[my_tile, 3:4, :] = 0.5 / (width * width)
     table[my_tile, 4:5, :] = wave * cos_turns(turns)
     table[my_tile, 5:6, :] = wave * cos_turns(turns - 0.25)
     table[my_tile, 6:7, :] = 2.0 * jnp.exp(level * math.log(1.5))
@@ -158,7 +161,7 @@
             delta_x = column(seg, 3 * route) - param(0)
             delta_y = column(seg, 3 * route + 1) - param(1)
             delta_t = column(seg, 3 * route + 2) - param(2)
-            envelope = jnp.exp2(
+            envelope = jnp.exp(
                 -(delta_x * delta_x + delta_y * delta_y) * param(3) - delta_t * delta_t
             )
             phi = envelope * root * cos_turns(delta_x * param(4) + delta_y * param(5))
@@ -211,33 +214,42 @@
         return tile, lambda row: table[tile, row : row + 1, :]
 
     def axis_factors(delta, inverse, wave_row):
-        envelope = jnp.exp2(-(delta * delta) * inverse)
+        envelope = jnp.exp(-(delta * delta) * inverse)
         phase = delta * wave_row
         return envelope * cos_turns(phase), envelope * cos_turns(phase - 0.25)
 
     def grid_factors_y():
         cell = lax.broadcasted_iota(jnp.int32, (LANES, LANES), 0) & (GY - 1)
         place_y = (cell.astype(jnp.float32) + 0.5) / GY
-        for neighbor in range(3):
+
+        def one(neighbor, carry):
             _, param = grid_params(neighbor)
             even, odd = axis_factors(place_y - param(1), param(3), param(5))
-            grid_y[neighbor, :, :LANES] = even
-            grid_y[neighbor, :, LANES:] = odd
+            for half, factor in enumerate((even, odd)):
+                high, low = split(factor)
+                grid_y[neighbor, 0, :, half * LANES : half * LANES + LANES] = high
+                grid_y[neighbor, 1, :, half * LANES : half * LANES + LANES] = low
+            return carry
+
+        lax.fori_loop(0, 3, one, 0)
 
     def grid_factors_x():
         row = lax.broadcasted_iota(jnp.int32, (GX, LANES), 0)
         cell = (row & 7) * (GX // 8) + (row >> 3)
         place_x = (cell.astype(jnp.float32) + 0.5) / GX
         day = (my_pass.astype(jnp.float32) + 0.5) / passes * TIME_SCALE
-        for neighbor in range(3):
+
+        def one(neighbor, carry):
             _, param = grid_params(neighbor)
-            even, odd = axis_factors(
-                place_x - (param(0) + float(neighbor - 1)), param(3), param(4)
-            )
+            side = (neighbor - 1).astype(jnp.float32)
+            even, odd = axis_factors(place_x - (param(0) + side), param(3), param(4))
             delta_t = day - param(2)
-            in_time = jnp.exp2(-(delta_t * delta_t))
+            in_time = jnp.exp(-(delta_t * delta_t))
             grid_x[neighbor, :, :LANES] = even * in_time
             grid_x[neighbor, :, LANES:] = -odd * in_time
+            return carry
+
+        lax.fori_loop(0, 3, one, 0)
 
     zeros = jnp.zeros((tiles, LANES), jnp.float32)
     rhs = all_sum(
@@ -262,21 +274,25 @@
     fields = []
 
     def grid_fields():
-        total = None
-        for neighbor in range(3):
+        def one(neighbor, total):
             tile, _ = grid_params(neighbor)
             parts = []
             for which in range(2):
                 row = vectors[which, pl.ds(tile, 1), :]
                 parts.append(grid_x[neighbor] * jnp.concatenate([row, row], axis=1))
-            term = lax.dot_general(
-                jnp.concatenate(parts, axis=0),
-                grid_y[neighbor],
-                (((1,), (1,)), ((), ())),
-                precision=HIGHEST,
-                preferred_element_type=jnp.float32,
+            high, low = split(jnp.concatenate(parts, axis=0))
+
+            def dot(left, right):
+                return lax.dot_general(
+                    left, right, (((1,), (1,)), ((), ())), preferred_element_type=jnp.float32
+                )
+
+            return total + (
+                dot(high, grid_y[neighbor, 0])
+                + (dot(high, grid_y[neighbor, 1]) + dot(low, grid_y[neighbor, 0]))
             )
-            total = term if total is None else total + term
+
+        total = lax.fori_loop(0, 3, one, jnp.zeros((2 * GX, LANES), jnp.float32))
         group = lax.broadcasted_iota(jnp.int32, (8, LANES), 1) // GY
         for begin in (0, GX):
             field = jnp.zeros((8, LANES), jnp.float32)
@@ -359,7 +375,7 @@
             pltpu.VMEM((seg_count * fan_out, seg_length, LANES), jnp.float32),
             pltpu.VMEM((2, tiles, LANES), jnp.float32),
             pltpu.VMEM((3, GX, 2 * LANES), jnp.float32),
-            pltpu.VMEM((3, LANES, 2 * LANES), jnp.float32),
+            pltpu.VMEM((3, 2, LANES, 2 * LANES), jnp.bfloat16),
             pltpu.VMEM((2, passes, tiles, LANES), jnp.float32),
             pltpu.VMEM((2, tiles, tiles, LANES), jnp.float32),
             pltpu.VMEM((tiles * passes, 1, LANES), jnp.float32),

time: 33.4 us -> 33.4 us (level)
  no operation moved by 1% of the time
where the time goes in v5:
time: 33.4 us; the launch traced here: 33.2 us
  Pallas kernels  32.6 us (98%)
  between operations  0.64 us (2%)
    pallas_call x1, Pallas kernels, on_device(): pl.pallas_call(functools.partial(kernel, tiles, passes), out_shape=(jax.S...  31.3 us
    pallas_call x1, Pallas kernels, on_device(): pl.pallas_call(hand_over, out_shape=(jax.ShapeDtypeStruct((1, LANES), jnp...  1.26 us

profile of v5, /device:TPU:0, one launch (start us, length us, event | category | flops | bytes accessed | tf_op | source)
XLA Modules:
  0.0 33.2 jit_solution(1576039951849605382)
XLA Ops:
  0.6 31.3 %shard_map.86 = (f32[1,128]{1,0:T(1,128)}, f32[8,128]{1,0:T(8,128)}) custom-call(f32[3,2,1024]{2,1,0:T(2,128)} %bitcast.9, f32[1,1024]{1,0:T(1,128)} %bitcast.10, f32[1,1024]{1,0:T(1,128)} %bitcast.11, s32[2,16]{1,0:T(2,128)} %bitcast.12, s32[1,128]{1,0:T(1,128)} %bitcast.13, s32[1,128]{1,0:T(1,128)} %bitcast.14, s32[1,128]{1,0:T(1,128)} %bitcast.15), custom_call_target="tpu_custom_call" | custom-call | tf_op jit(solution)/shard_map/pallas_call | solution.py:355
  32.0 1.3 %shard_map.87 = (f32[1,128]{1,0:T(1,128)}, f32[8,128]{1,0:T(8,128)}) custom-call(f32[1,128]{1,0:T(1,128)} %get-tuple-element.6.coef_in, f32[8,128]{1,0:T(8,128)} %get-tuple-element.7.field_in), custom_call_target="tpu_custom_call" | custom-call | tf_op jit(solution)/shard_map/pallas_call | solution.py:400

commit v6 on v3

--- a/solution.py
+++ b/solution.py
@@ -60,7 +60,7 @@
     coef_ref, field_ref,
     obs_ref, value_ref, weight_ref, seg_ref, scale_ref, orient_ref, place_ref, input_sems,
     table, stack, wide, basis, vectors, grid_x, grid_y,
-    near, far, last, table_sems, near_sems, far_sems, last_sems,
+    near, far, last_near, last_far, table_sems, near_sems, far_sems,
 ):
     my_tile, my_pass = lax.axis_index("tile"), lax.axis_index("pass")
     fan_out, seg_count = seg_ref.shape
@@ -289,25 +289,12 @@
     energies = lax.fori_loop(
         0, seg_count, energy, jnp.zeros((seg_length, 1), jnp.float32), unroll=8
     )
-    me, everyone = my_tile * passes + my_pass, tiles * passes
-
-    def to_anyone(distance):
-        other = lax.rem(me + distance, everyone)
-        return pltpu.make_async_remote_copy(
-            src_ref=last.at[me],
-            dst_ref=last.at[me],
-            send_sem=last_sems.at[0],
-            recv_sem=last_sems.at[1],
-            device_id={"tile": other // passes, "pass": lax.rem(other, passes)},
-            device_id_type=MESH,
-        )
-
-    last[me] = jnp.broadcast_to(jnp.sum(energies, axis=0, keepdims=True), (1, LANES))
-    peers(everyone, lambda d: to_anyone(d).start())
-    grid_fields()
-    prior_product = total_of(direction * direction * prior)
-    wait_for_peers(last, everyone, last_sems.at[1])
-    product = jnp.sum(last[:, 0, :], axis=0, keepdims=True)[:, 0:1] + prior_product
+    parts = []
+    product = all_sum(
+        jnp.broadcast_to(jnp.sum(energies, axis=0, keepdims=True), (1, LANES)),
+        last_near, last_far, near_sems.at[2], far_sems.at[2],
+        (lambda: parts.append(total_of(direction * direction * prior)), grid_fields),
+    )[:, 0:1] + parts[0]
     step_second = norm_next / product
     mine = pl.ds(my_tile, 1)
     coef_ref[...] = step_first * vectors[0, mine, :] + step_second * vectors[1, mine, :]
@@ -317,7 +304,8 @@
     for stage in range(2):
         wait_for_peers(near.at[stage], passes, near_sems.at[stage, 0])
         wait_for_peers(far.at[stage], tiles, far_sems.at[stage, 0])
-    wait_for_peers(last, everyone, last_sems.at[0])
+    wait_for_peers(last_near, passes, near_sems.at[2, 0])
+    wait_for_peers(last_far, tiles, far_sems.at[2, 0])
 
 
 def hand_over(coef_in, field_in, coef_ref, field_ref, sems):
@@ -362,11 +350,11 @@
             pltpu.VMEM((3, LANES, 2 * LANES), jnp.float32),
             pltpu.VMEM((2, passes, tiles, LANES), jnp.float32),
             pltpu.VMEM((2, tiles, tiles, LANES), jnp.float32),
-            pltpu.VMEM((tiles * passes, 1, LANES), jnp.float32),
+            pltpu.VMEM((passes, 1, LANES), jnp.float32),
+            pltpu.VMEM((tiles, 1, LANES), jnp.float32),
             pltpu.SemaphoreType.DMA((2,)),
-            pltpu.SemaphoreType.DMA((2, 2)),
-            pltpu.SemaphoreType.DMA((2, 2)),
-            pltpu.SemaphoreType.DMA((2,)),
+            pltpu.SemaphoreType.DMA((3, 2)),
+            pltpu.SemaphoreType.DMA((3, 2)),
         ],
         compiler_params=pltpu.CompilerParams(
             collective_id=0, has_side_effects=True, vmem_limit_bytes=60 * 2**20

time: 33.4 us -> 35.5 us (1.063)
  Pallas kernels: 32.6 us -> 34.6 us
    pallas_call x1, Pallas kernels: 31.3 us -> 33.4 us  [on_device(): pl.pallas_call(functools.partial(kernel, tiles, passes), out_shape=(jax.S...]
where the time goes in v6:
time: 35.5 us; the launch traced here: 35.3 us
  Pallas kernels  34.6 us (97%)
  between operations  0.64 us (2%)
    pallas_call x1, Pallas kernels, on_device(): pl.pallas_call(functools.partial(kernel, tiles, passes), out_shape=(jax.S...  33.4 us
    pallas_call x1, Pallas kernels, on_device(): pl.pallas_call(hand_over, out_shape=(jax.ShapeDtypeStruct((1, LANES), jnp...  1.26 us

profile of v6, /device:TPU:0, one launch (start us, length us, event | category | flops | bytes accessed | tf_op | source)
XLA Modules:
  0.0 35.3 jit_solution(3797360571845249404)
XLA Ops:
  0.6 33.4 %shard_map.86 = (f32[1,128]{1,0:T(1,128)}, f32[8,128]{1,0:T(8,128)}) custom-call(f32[3,2,1024]{2,1,0:T(2,128)} %bitcast.9, f32[1,1024]{1,0:T(1,128)} %bitcast.10, f32[1,1024]{1,0:T(1,128)} %bitcast.11, s32[2,16]{1,0:T(2,128)} %bitcast.12, s32[1,128]{1,0:T(1,128)} %bitcast.13, s32[1,128]{1,0:T(1,128)} %bitcast.14, s32[1,128]{1,0:T(1,128)} %bitcast.15), custom_call_target="tpu_custom_call" | custom-call | tf_op jit(solution)/shard_map/pallas_call | solution.py:327
  34.0 1.3 %shard_map.87 = (f32[1,128]{1,0:T(1,128)}, f32[8,128]{1,0:T(8,128)}) custom-call(f32[1,128]{1,0:T(1,128)} %get-tuple-element.6.coef_in, f32[8,128]{1,0:T(8,128)} %get-tuple-element.7.field_in), custom_call_target="tpu_custom_call" | custom-call | tf_op jit(solution)/shard_map/pallas_call | solution.py:372
